TPU v7x, 256 devices: a whole 4x4x8 slice. The times are simulated.
256 devices in a mesh: pole: 4 (over x), row: 8 (over z_hi, core), col: 8 (over y, z_lo).
Axes of the slice: x: 4, y: 4, z: 8 (z_hi: 4, z_lo: 2; z = z_hi * 2 + z_lo), core: 2. Of those that a mesh axis runs over, the one named last changes fastest.
Arguments:
- root_inverse: float32 [4, 2, 4096, 4096], P('pole', None, 'row', 'col'), may hold values from -0.09375 to 0.09375
- panel: float32 [4, 2048, 2, 4096], P('pole', 'col', None, 'row'), may hold values from -2 to 2
- diag_inverse: float32 [4, 16, 2, 128, 128], P('pole', 'col'), may hold values from -4 to 4
- pole_weight: float32 [4, 2], P('pole'), may hold values from -3 to 3
- block_node: int32 [16], P('col'), may hold values from 0 to 3, as said below
- pattern: int32 [4, 32], P(None, 'row'), may hold values 0 or 1
Outputs:
- density_panel: float32 [2048, 4096], P('col', 'row')
- density_tiles: float32 [16, 128, 128], P('col')
Inputs may be any that keep to these rules, and one draw needn't show every extreme that they name: `block_node`: each child supernode covers consecutive blocks, at least one and at most 8; one covers exactly 8.
All inputs are finite; a program needn't handle non-finite values. No bound on the sum of `pattern` on one device may be relied on, other than what follows from the above.
Results may differ from a plain program's by a relative error of at most 0.0001.
Values sent between devices are 32-bit elements; how exact they have to be, the bound alone decides.
A program may use at most 128 MiB of HBM per device.

v0:
```python
import jax
import jax.numpy as jnp
from jax import lax
from jax.sharding import PartitionSpec as P

TILE = 128
NODES = 4


def contract(left, right):
    dims = (((1,), (1,)), ((), ()))
    return lax.dot_general(
        left, right, dims, precision=lax.Precision.HIGHEST, preferred_element_type=jnp.float32
    )


def apply_inverse(left_real, left_imag, inv_real, inv_imag):
    real_part = contract(left_real, inv_real) - contract(left_imag, inv_imag)
    imag_part = contract(left_imag, inv_real) + contract(left_real, inv_imag)
    return jnp.stack([real_part, imag_part], axis=1)


def tile_product(left, right):
    return jnp.einsum("tak,tbk->tab", left, right, precision=lax.Precision.HIGHEST)


def shards(root_inverse, panel, diag_inverse, pole_weight, block_node, pattern):
    local_rows = panel.shape[3]
    local_blocks = block_node.shape[0]
    node_hot = (block_node[:, None] == jnp.arange(NODES, dtype=jnp.int32)[None, :]).astype(
        jnp.float32
    )
    block_mask = jnp.dot(node_hot, pattern.astype(jnp.float32), precision=lax.Precision.HIGHEST)
    full_mask = jnp.repeat(jnp.repeat(block_mask, TILE, axis=0), TILE, axis=1)
    masked = panel[0] * full_mask[:, None, :]
    gathered = lax.all_gather(masked, "row", axis=2, tiled=True)
    portion = lax.all_gather(root_inverse, "col", axis=3, tiled=True)
    product = apply_inverse(gathered[:, 0], gathered[:, 1], portion[0, 0], portion[0, 1])
    weight_real = pole_weight[0, 0]
    weight_imag = pole_weight[0, 1]
    panel_term = -(weight_real * product[:, 0] - weight_imag * product[:, 1]) * full_mask
    dens_panel = lax.psum(panel_term, "pole")
    tiled_left = masked.reshape(local_blocks, TILE, 2, local_rows)
    tiled_right = product.reshape(local_blocks, TILE, 2, local_rows)
    coupling_real = tile_product(tiled_left[:, :, 0], tiled_right[:, :, 0]) - tile_product(
        tiled_left[:, :, 1], tiled_right[:, :, 1]
    )
    coupling_imag = tile_product(tiled_left[:, :, 0], tiled_right[:, :, 1]) + tile_product(
        tiled_left[:, :, 1], tiled_right[:, :, 0]
    )
    diag_block = diag_inverse[0]
    summed_real, summed_imag = lax.psum((coupling_real, coupling_imag), "row")
    tile_term = weight_real * (diag_block[:, 0] + summed_real) - weight_imag * (
        diag_block[:, 1] + summed_imag
    )
    dens_tiles = lax.psum(tile_term, "pole")
    return (dens_panel, dens_tiles)


def solution(mesh):
    placed = (
        P("pole", None, "row", "col"),
        P("pole", "col", None, "row"),
        P("pole", "col", None, None, None),
        P("pole", None),
        P("col"),
        P(None, "row"),
    )
    return jax.shard_map(
        shards,
        mesh=mesh,
        in_specs=placed,
        out_specs=(P("col", "row"), P("col", None, None)),
        check_vma=False,
    )
```

profile of v0, /device:TPU:1, one launch (start us, length us, event | category | flops | bytes accessed | tf_op | source)
XLA Modules:
  0.0 616.5 jit_solution(5836406628777120039)
XLA Ops:
  7.2 0.9 fusion.25
  8.1 0.3 broadcast_in_dim.9
  8.5 2.9 bitcast_multiply_fusion
  11.4 0.7 all-gather.5.cloned.1.call-update
  12.2 0.2 mul.53
  12.4 0.2 copy.9
  12.6 0.6 fusion.31
  13.2 0.1 broadcast_multiply_fusion
  13.4 95.2 %all-gather.3.cloned.1.call-done = f32[256,2,4096]{2,1,0:T(2,128)} async-done(((f32[256,2,512]{2,1,0:T(2,128)}), f32[256,2,4096]{2,1,0:T(2,128)}) %all-gather.3.cloned.1.call-update) | async-done | bytes 8388624 | tf_op jit(solution)/shard_map/all_gather | solution.py:36
  108.6 12.3 %fusion.30 = (f32[256,1,4096]{2,1,0:T(1,128)}, f32[256,1,4096]{2,1,0:T(1,128)}) fusion(f32[256,2,4096]{2,1,0:T(2,128)} %all-gather.3.cloned.1.call-done), kind=kLoop, calls=%fused_computation.39 | loop fusion | bytes 16777216 | tf_op jit(solution)/shard_map/slice | solution.py:38
  120.8 315.5 %all-gather.5.cloned.1.call-done = f32[1,2,512,4096]{3,2,1,0:T(8,128)} async-done(((f32[1,2,512,512]{3,2,1,0:T(8,128)}), f32[1,2,512,4096]{3,2,1,0:T(8,128)}) %all-gather.5.cloned.1.call-update) | async-done | bytes 16777232 | tf_op jit(solution)/shard_map/all_gather | solution.py:37
  436.3 11.4 %fusion.1 = f32[256,512]{1,0:T(8,128)S(1)} fusion(f32[1,2,512,4096]{3,2,1,0:T(8,128)} %all-gather.5.cloned.1.call-done, f32[256,1,4096]{2,1,0:T(1,128)} %get-tuple-element.6), kind=kOutput, calls=%fused_computation.3 | convolution fusion | flops 6442450944 | bytes 13107200 | tf_op jit(solution)/shard_map/dot_general | solution.py:12
  447.8 11.7 %fusion.12 = f32[256,512]{1,0:T(8,128)S(1)} fusion(f32[256,512]{1,0:T(8,128)S(1)} %fusion.1, f32[1,2,512,4096]{3,2,1,0:T(8,128)} %all-gather.5.cloned.1.call-done, f32[256,1,4096]{2,1,0:T(1,128)} %get-tuple-element.7), kind=kOutput, calls=%fused_computation.14 | convolution fusion | flops 6442582016 | bytes 13631488 | tf_op jit(solution)/shard_map/dot_general | solution.py:12
  459.4 0.6 fusion.19
  460.1 9.3 %fusion = f32[256,512]{1,0:T(8,128)S(1)} fusion(f32[1,2,512,4096]{3,2,1,0:T(8,128)S(1)} %copy-done, f32[256,1,4096]{2,1,0:T(1,128)S(1)} %copy-done.1), kind=kOutput, calls=%fused_computation.2 | convolution fusion | flops 6442450944 | bytes 13107200 | tf_op jit(solution)/shard_map/dot_general | solution.py:12
  469.4 11.6 %negate_multiply_fusion = (f32[256,512]{1,0:T(8,128)}, f32[256,512]{1,0:T(8,128)S(1)}) fusion(f32[256,512]{1,0:T(8,128)S(1)} %fusion.12, f32[]{:T(128)} %bitcast.5, f32[]{:T(128)} %bitcast, f32[32,8,4,128]{3,2,1,0:T(4,128)S(1)} %bitcast.76, f32[256,512]{1,0:T(8,128)S(1)} %fusion, f32[1,2,512,4096]{3,2,1,0:T(8,128)S(1)} %copy-done, ...), kind=kOutput, calls=%fused_computation.23 | convolution fusion | flops 6443237376 | bytes 15204360 | tf_op jit(solution)/shard_map/dot_general | solution.py:12
  481.0 0.6 fusion.18
  481.7 1.3 convolution_subtract_fusion
  483.0 1.3 convolution_add_fusion
  484.4 73.0 %all-reduce.5.cloned.1.call-done = (f32[2,128,128]{2,1,0:T(8,128)}, f32[2,128,128]{2,1,0:T(8,128)}) async-done(((f32[2,128,128]{2,1,0:T(8,128)}, f32[2,128,128]{2,1,0:T(8,128)}), (f32[2,128,128]{2,1,0:T(8,128)}, f32[2,128,128]{2,1,0:T(8,128)})) %all-reduce.5.cloned.1.call-update) | async-done | bytes 262160 | tf_op jit(solution)/shard_map/psum | solution.py:52
  557.4 2.9 fusion.22
  560.2 46.3 %all-reduce.7.cloned.1.call-done = (f32[256,512]{1,0:T(8,128)}, f32[2,128,128]{2,1,0:T(8,128)}) async-done(((f32[256,512]{1,0:T(8,128)}, f32[2,128,128]{2,1,0:T(8,128)}), (f32[256,512]{1,0:T(8,128)}, f32[2,128,128]{2,1,0:T(8,128)})) %all-reduce.7.cloned.1.call-update) | async-done | bytes 655376 | tf_op jit(solution)/shard_map/psum | solution.py:42
  606.5 1.9 copy.45
  608.4 1.6 copy.46
  (22 shorter events, 0.3 us)
Async XLA Ops:
  7.2 101.4 %all-gather.3.cloned.1.call-start = ((), (), s32[]{:S(2)}) async-start(), calls=%async_computation | async-start | bytes 9437184 | tf_op jit(solution)/shard_map/all_gather | solution.py:36
  8.1 4.3 copy-start.3
  8.5 4.1 copy-start.5
  11.4 424.9 %all-gather.5.cloned.1.call-start = ((), (), s32[]{:S(2)}) async-start(), calls=%async_computation.1 | async-start | bytes 18874368 | tf_op jit(solution)/shard_map/all_gather | solution.py:37
  12.1 545.2 %all-reduce.5.cloned.1.call-start = ((), (), s32[]{:S(2)}) async-start(), calls=%async_computation.2 | async-start | bytes 524288 | tf_op jit(solution)/shard_map/psum | solution.py:52
  436.3 23.7 %copy-start = (f32[1,2,512,4096]{3,2,1,0:T(8,128)S(1)}, f32[1,2,512,4096]{3,2,1,0:T(8,128)}, u32[]{:S(2)}) copy-start(f32[1,2,512,4096]{3,2,1,0:T(8,128)} %all-gather.5.cloned.1.call-done) | copy-start | bytes 50331652
  447.8 12.3 %copy-start.1 = (f32[256,1,4096]{2,1,0:T(1,128)S(1)}, f32[256,1,4096]{2,1,0:T(1,128)}, u32[]{:S(2)}) copy-start(f32[256,1,4096]{2,1,0:T(1,128)} %get-tuple-element.7) | copy-start | bytes 12582916
  460.1 9.3 %copy-start.2 = (f32[256,1,4096]{2,1,0:T(1,128)S(1)}, f32[256,1,4096]{2,1,0:T(1,128)}, u32[]{:S(2)}) copy-start(f32[256,1,4096]{2,1,0:T(1,128)} %get-tuple-element.6) | copy-start | bytes 12582916
  481.0 3.3 copy-start.4
  484.3 122.2 %all-reduce.7.cloned.1.call-start = ((), (), s32[]{:S(2)}) async-start(), calls=%async_computation.3 | async-start | bytes 1310720 | tf_op jit(solution)/shard_map/psum | solution.py:42
Sparse Core Ops, SparseCore 0:
  11.5 97.0 all-gather.2
  110.4 325.9 all-gather.4
  484.4 72.9 all-reduce.4
  560.4 46.0 all-reduce.6
where the time goes:
time: 618 us; the launch traced here: 616 us
  waiting for transfers between devices  531 us (86%)
  matrix products  48.7 us (8%)
  local copies, waits for them, and re-layouts  17.1 us (3%)
  between operations  13.9 us (2%)
    all_gather x1, waiting for transfers between devices, shards(): portion = lax.all_gather(root_inverse, 'col', axis=3, tiled=True)  315 us
    all_gather x1, waiting for transfers between devices, shards(): gathered = lax.all_gather(masked, 'row', axis=2, tiled=True)  95.2 us
    psum x1, waiting for transfers between devices, shards(): summed_real, summed_imag = lax.psum((coupling_real, coupling_imag), 'row')  73 us
    psum x1, waiting for transfers between devices, shards(): dens_panel = lax.psum(panel_term, 'pole')  46.3 us
    dot_general x4, matrix products, contract(): lax.dot_general(left, right, dims, precision=lax.Precision.HIGHEST, prefe...  44 us
  transfers between devices with their start and end apart: 4, of which 4 were waited for; matrix products, arithmetic and copies ran while one was open for 2% of the time, Pallas kernels for 0%

commit v1 on v0

v1 whole, which is shorter than its diff:
```python
import jax
import jax.numpy as jnp
from jax import lax
from jax.experimental import pallas as pl
from jax.experimental.pallas import tpu as pltpu
from jax.sharding import PartitionSpec as P

TILE = 128
NODES = 4
MESH = pl.DeviceIdType.MESH
HIGHEST = lax.Precision.HIGHEST
NT = (((1,), (1,)), ((), ()))
VMEM_LIMIT = 56 * 1024 * 1024


def wrap(index):
    return lax.rem(index + 8, 4)


def dot(left, right, precision=None):
    return lax.dot_general(left, right, NT, precision=precision, preferred_element_type=jnp.float32)


def split(value):
    high = value.astype(jnp.bfloat16)
    return high, (value - high.astype(jnp.float32)).astype(jnp.bfloat16)


def kernel(
    inv, pan, diag, mask, weight, dens, tiles,
    inv_all, pan_all, inv_split, pan_split, total, partial, pieces, summed, tile_parts,
    inv_send, inv_recv, pan_send, pan_recv, red_send, red_recv, tile_send, tile_recv,
    out_send, out_recv, tout_send, tout_recv, own_sem,
):
    p = lax.axis_index("pole")
    row = lax.axis_index("row")
    col = lax.axis_index("col")
    h, c = row // 2, row % 2
    y, l = col // 2, col % 2

    def at(p_, h_, c_, y_, l_):
        return (p_, 2 * h_ + c_, 2 * y_ + l_)

    def remote(source, target, send, recv, device):
        return pltpu.make_async_remote_copy(
            src_ref=source, dst_ref=target, send_sem=send, recv_sem=recv,
            device_id=device, device_id_type=MESH,
        )

    sibling = at(p, h, 1 - c, y, l)
    up, down = at(p, h, c, wrap(y + 1), l), at(p, h, c, wrap(y - 1), l)
    others = [at(p, wrap(h + d), k, y, l) for d in (1, 2, 3) for k in (0, 1)] + [sibling]
    reducers = [(wrap(p + d), (l + e) % 2) for d in range(4) for e in range(2)]

    barrier = pltpu.get_barrier_semaphore()
    greeted = [up, down] + others
    greeted += [at(p, wrap(h + l), k, y, 1 - l) for k in (0, 1)]
    greeted += [at(p, wrap(h - 1 + l), k, y, 1 - l) for k in (0, 1)]
    greeted += [at(wrap(p + d), h, c, y, k) for d in (1, 2, 3) for k in (0, 1)]
    for device in greeted:
        pl.semaphore_signal(barrier, inc=1, device_id=device, device_id_type=MESH)
    pl.semaphore_wait(barrier, len(greeted))

    started = []

    def send(*args):
        copy = remote(*args)
        copy.start()
        started.append(copy)

    first = [(0, up), (1, down), (1, up), (0, down)]
    own_slot = 2 * h + l
    same = 1 - (c - l) * (c - l)
    cross = 1 - same
    right_h = wrap(h + same + cross * l)
    left_h = wrap(h - 1 + cross * l)

    def send_inv(k):
        part, device = first[k]
        send(inv.at[part], inv_all.at[y, part], inv_send.at[k], inv_recv.at[y, part], device)

    def send_pan(k, half, h_):
        send(pan.at[half], pan_all.at[own_slot, half], pan_send.at[k], pan_recv.at[own_slot, half],
             at(p, h_, half, y, c))

    send_inv(0)
    send_inv(1)
    send_pan(0, 0, right_h)
    send_pan(1, 1, left_h)
    send_pan(2, 1, right_h)
    send_pan(3, 0, left_h)
    send_inv(2)
    send_inv(3)

    def shared(half):
        return remote(pan.at[half], pan_all.at[own_slot, half], pan_send.at[4 + half],
                      pan_recv.at[own_slot, half], sibling)

    def crossed(half):
        return remote(pan.at[half], pan_all.at[8, half], pan_send.at[6 + half],
                      pan_recv.at[8, half], at(p, h, c, y, 1 - l))

    @pl.when(same == 1)
    def _():
        for half in (0, 1):
            shared(half).start()
            pltpu.make_async_copy(pan.at[half], pan_all.at[own_slot, half], pan_recv.at[own_slot, half]).start()
        for half in (0, 1):
            crossed(half).start()

    own_inv = pltpu.make_async_copy(inv, inv_all.at[y], own_sem)
    own_inv.start()

    def arrived_inv(k, part):
        remote(inv.at[part], inv_all.at[k, part], inv_send.at[0], inv_recv.at[k, part], up).wait_recv()

    def arrived_pan(slot, half):
        remote(pan.at[half], pan_all.at[slot, half], pan_send.at[0], pan_recv.at[slot, half], sibling).wait_recv()

    y_left, y_right = wrap(y - 1), wrap(y + 1)
    cross_left = 2 * wrap(h - 1 + l) + 1 - l
    cross_right = 2 * wrap(h + l) + 1 - l
    same_left = 2 * wrap(h - 1) + l
    same_right = 2 * wrap(h + 1) + l
    far_left = 2 * wrap(h - 2 + l) + 1 - l
    far_right = 2 * wrap(h + 1 + l) + 1 - l
    same_far = 2 * wrap(h + 2) + l
    on_right, on_left = at(p, wrap(h + 1), c, y, l), at(p, wrap(h - 1), c, y, l)

    def pass_pan(k, slot, device):
        send(pan_all.at[slot, c], pan_all.at[slot, c], pan_send.at[k], pan_recv.at[slot, c], device)

    arrived_pan(cross_left, c)
    pass_pan(8, cross_left, on_right)
    pass_pan(9, cross_left, sibling)
    arrived_pan(cross_right, c)
    pass_pan(10, cross_right, on_left)
    pass_pan(11, cross_right, sibling)
    arrived_inv(y_left, 0)
    send(inv_all.at[y_left, 0], inv_all.at[y_left, 0], inv_send.at[4], inv_recv.at[y_left, 0], up)
    arrived_inv(y_right, 1)
    send(inv_all.at[y_right, 1], inv_all.at[y_right, 1], inv_send.at[5], inv_recv.at[y_right, 1], down)
    arrived_pan(same_left, c)
    arrived_pan(same_right, c)
    pass_pan(12, (1 - c) * same_left + c * same_right, at(p, wrap(h + 1 - 2 * c), c, y, l))
    pass_pan(13, same_left, sibling)
    pass_pan(14, same_right, sibling)

    own_inv.wait()
    arrived_pan(own_slot * same + (2 * h + l) * cross, 0)
    arrived_pan(own_slot * same + (2 * h + l) * cross, 1)
    for slot in (cross_left, cross_right, same_left, same_right):
        arrived_pan(slot, 1 - c)
    arrived_inv(y_left, 1)
    arrived_inv(y_right, 0)

    def multiply(k, fresh):
        def take(step, _):
            rows = pl.ds(pl.multiple_of(step * TILE, TILE), TILE)
            for part in (0, 1):
                high, low = split(inv_all[k, part, rows, :])
                inv_split[part, 0, rows, :] = high
                inv_split[part, 1, rows, :] = low
                high, low = split(pan_all[2 * k + step // 2, step % 2, part])
                pan_split[part, 0, rows, :] = high
                pan_split[part, 1, rows, :] = low
            return 0

        lax.fori_loop(0, 4, take, 0)

        def add(step, _):
            rows = pl.ds(pl.multiple_of(step * 256, 256), 256)

            def three(left, right):
                return (
                    dot(pan_split[left, 0], inv_split[right, 0, rows, :])
                    + dot(pan_split[left, 0], inv_split[right, 1, rows, :])
                    + dot(pan_split[left, 1], inv_split[right, 0, rows, :])
                )

            real = three(0, 0) - three(1, 1)
            imag = three(1, 0) + three(0, 1)
            if fresh:
                total[0, :, rows] = real
                total[1, :, rows] = imag
            else:
                total[0, :, rows] += real
                total[1, :, rows] += imag
            return 0

        lax.fori_loop(0, 2, add, 0)

    apart = (1 - lax.rem(h - y + 8, 2)) * (lax.rem(h - y + 8, 4) // 2)
    begin = wrap(h + apart * (2 * l - 1))
    multiply(begin, True)

    for k, slot in ((15, far_left), (16, far_right), (17, same_far)):
        arrived_pan(slot, c)
        pass_pan(k, slot, sibling)
    y_far = wrap(y + 2)
    arrived_inv(y_far, 0)
    arrived_inv(y_far, 1)
    for slot in (far_left, far_right, same_far):
        arrived_pan(slot, 1 - c)

    @pl.when(same == 0)
    def _():
        arrived_pan(8, 0)
        arrived_pan(8, 1)

    for d in (1, 2, 3):
        multiply(wrap(begin + d), False)

    real_weight = weight[0, 0]
    imag_weight = weight[0, 1]
    other = same * (2 * h + 1 - l) + cross * 8
    here = ((7 - row) // 7).astype(jnp.float32)
    for o in (0, 1):
        for half in (0, 1):
            begin_row = (l if o == 0 else 1 - l) * 256 + half * TILE
            rows = pl.ds(pl.multiple_of(begin_row, TILE), TILE)
            real = total[0, rows, :]
            imag = total[1, rows, :]
            weighted_real = real_weight * real - imag_weight * imag
            weighted_imag = real_weight * imag + imag_weight * real
            if o == 0:
                left_real, left_imag = pan[half, 0], pan[half, 1]
            else:
                left_real, left_imag = pan_all[other, half, 0], pan_all[other, half, 1]
            tile = dot(left_real, weighted_real, HIGHEST) - dot(left_imag, weighted_imag, HIGHEST)
            if o == 0:
                tile += here * (real_weight * diag[half, 0] - imag_weight * diag[half, 1])
            partial[rows, 0:512] = weighted_real
            partial[rows, 512:640] = tile

    me = 2 * p + l

    def piece(p_, l_):
        return pl.ds(pl.multiple_of(l_ * 256 + p_ * 64, 64), 64)

    for k in range(1, 8):
        p_, l_ = reducers[k]
        send(partial.at[piece(p_, l_)], pieces.at[me], red_send.at[k], red_recv.at[me], at(p_, h, c, y, l_))
    for k in range(1, 8):
        p_, l_ = reducers[k]
        remote(partial.at[piece(p_, l_)], pieces.at[2 * p_ + l_], red_send.at[k],
               red_recv.at[2 * p_ + l_], sibling).wait_recv()
    summed[...] = partial[piece(p, l), :]
    for k in range(1, 8):
        p_, l_ = reducers[k]
        summed[...] += pieces[2 * p_ + l_]

    tile_parts[row] = summed[:, 512:640]
    for k, device in enumerate(others):
        send(tile_parts.at[row], tile_parts.at[row], tile_send.at[k], tile_recv.at[row], device)
    mine = pl.ds(pl.multiple_of(p * 64, 64), 64)
    for j in range(4):
        dens[mine, j * TILE:(j + 1) * TILE] = -mask[p // 2, j] * summed[:, j * TILE:(j + 1) * TILE]
    for d in (1, 2, 3):
        send(dens.at[mine], dens.at[mine], out_send.at[d], out_recv.at[p], at(wrap(p + d), h, c, y, l))
    for k in range(1, 8):
        slot = lax.rem(row + k, 8)
        remote(tile_parts.at[slot], tile_parts.at[slot], tile_send.at[0], tile_recv.at[slot], sibling).wait_recv()
    whole = tile_parts[0]
    for k in range(1, 8):
        whole += tile_parts[k]
    tiles[mine, :] = whole
    for d in (1, 2, 3):
        send(tiles.at[mine], tiles.at[mine], tout_send.at[d], tout_recv.at[p], at(wrap(p + d), h, c, y, l))
    for d in (1, 2, 3):
        p_ = wrap(p + d)
        theirs = pl.ds(pl.multiple_of(p_ * 64, 64), 64)
        remote(dens.at[theirs], dens.at[theirs], out_send.at[0], out_recv.at[p_], sibling).wait_recv()
        remote(tiles.at[theirs], tiles.at[theirs], tout_send.at[0], tout_recv.at[p_], sibling).wait_recv()

    for copy in started:
        copy.wait_send()

    @pl.when(same == 1)
    def _():
        for half in (0, 1):
            shared(half).wait_send()
            crossed(half).wait_send()


def shards(root_inverse, panel, diag_inverse, pole_weight, block_node, pattern):
    node_hot = (block_node[:, None] == jnp.arange(NODES, dtype=jnp.int32)[None, :]).astype(jnp.float32)
    block_mask = jnp.sum(node_hot[:, :, None] * pattern.astype(jnp.float32)[None], axis=1)
    cut = panel[0].reshape(2, TILE, 2, 4, TILE) * block_mask[:, None, None, :, None]
    cut = cut.transpose(0, 2, 1, 3, 4).reshape(2, 2, TILE, 512)
    dma = pltpu.SemaphoreType.DMA
    vmem = pl.BlockSpec(memory_space=pltpu.VMEM)
    smem = pl.BlockSpec(memory_space=pltpu.SMEM)
    dens, tiles = pl.pallas_call(
        kernel,
        out_shape=(
            jax.ShapeDtypeStruct((256, 512), jnp.float32),
            jax.ShapeDtypeStruct((256, TILE), jnp.float32),
        ),
        in_specs=[pl.BlockSpec(memory_space=pl.ANY), vmem, vmem, smem, smem],
        out_specs=(vmem, vmem),
        scratch_shapes=[
            pltpu.VMEM((4, 2, 512, 512), jnp.float32),
            pltpu.VMEM((9, 2, 2, TILE, 512), jnp.float32),
            pltpu.VMEM((2, 2, 512, 512), jnp.bfloat16),
            pltpu.VMEM((2, 2, 512, 512), jnp.bfloat16),
            pltpu.VMEM((2, 512, 512), jnp.float32),
            pltpu.VMEM((512, 640), jnp.float32),
            pltpu.VMEM((8, 64, 640), jnp.float32),
            pltpu.VMEM((64, 640), jnp.float32),
            pltpu.VMEM((8, 64, TILE), jnp.float32),
            dma((6,)), dma((4, 2)),
            dma((18,)), dma((9, 2)),
            dma((8,)), dma((8,)),
            dma((7,)), dma((8,)),
            dma((4,)), dma((4,)),
            dma((4,)), dma((4,)),
            dma,
        ],
        compiler_params=pltpu.CompilerParams(
            collective_id=0, has_side_effects=True, vmem_limit_bytes=VMEM_LIMIT
        ),
        cost_estimate=pl.CostEstimate(flops=26_000_000_000, bytes_accessed=6_000_000, transcendentals=0),
    )(root_inverse[0], cut, diag_inverse[0], block_mask, pole_weight)
    return dens, tiles.reshape(2, TILE, TILE)


def solution(mesh):
    placed = (
        P("pole", None, "row", "col"),
        P("pole", "col", None, "row"),
        P("pole", "col", None, None, None),
        P("pole", None),
        P("col"),
        P(None, "row"),
    )
    return jax.shard_map(
        shards,
        mesh=mesh,
        in_specs=placed,
        out_specs=(P("col", "row"), P("col", None, None)),
        check_vma=False,
    )
```

time: 618 us -> 148 us (0.24)
  waiting for transfers between devices: 531 us -> 0 us
  Pallas kernels: 0 us -> 138 us
  matrix products: 48.7 us -> 0 us
  between operations: 13.9 us -> 0.66 us
  local copies, waits for them, and re-layouts: 17.1 us -> 7.09 us
    all_gather x2 -> x0, waiting for transfers between devices: 411 us -> none  [the longest x1 315 us: shards(): portion = lax.all_gather(root_inverse, 'col', axis=3, tiled=True)]
    pallas_call x0 -> x1, Pallas kernels: none -> 138 us  [shards(): pl.pallas_call(kernel, out_shape=(jax.ShapeDtypeStruct((256, 512), jnp.fl...]
    psum x2 -> x0, waiting for transfers between devices: 119 us -> none  [the longest x1 73 us: shards(): summed_real, summed_imag = lax.psum((coupling_real, coupling_imag), 'row')]
    dot_general x9 -> x0, matrix products: 48.7 us -> none  [the longest x4 44 us: contract(): lax.dot_general(left, right, dims, precision=lax.Precision.HIGHEST, prefe...]
    slice x2 -> x0, local copies, waits for them, and re-layouts: 12.9 us -> none  [the longest x1 12.3 us: shards(): gathered[:, 0]]
  transfers between devices with their start and end apart: 4 -> 0, of which waited for: 4 -> 0; matrix products, arithmetic and copies ran while one was open for 2% -> 0% of each run, Pallas kernels for 0% -> 0%
where the time goes in v1:
time: 148 us
  Pallas kernels  138 us (93%)
  local copies, waits for them, and re-layouts  7.09 us (5%)
  other arithmetic  1.74 us (1%)
    pallas_call x1, Pallas kernels, shards(): pl.pallas_call(kernel, out_shape=(jax.ShapeDtypeStruct((256, 512), jnp.fl...  138 us
    unnamed x4, local copies, waits for them, and re-layouts  3.44 us

profile of v1, /device:TPU:1, one launch (start us, length us, event | category | flops | bytes accessed | tf_op | source)
XLA Modules:
  0.0 147.6 jit_solution(6955546262618064674)
XLA Ops:
  0.6 0.7 compare_convert_fusion
  1.4 0.7 convert_element_type.11
  2.0 0.1 multiply_reduce_fusion.mask
  2.1 0.0 copy-start
  2.1 2.2 %reshape_squeeze.3 = f32[2,128,2,4,128]{4,3,2,1,0:T(4,128)S(1)} reshape(f32[1,256,2,512]{3,2,1,0:T(2,128)} %param.7) | data formatting | bytes 2097152 | tf_op jit(solution)/shard_map/reshape;squeeze | solution.py:289
  4.4 0.2 fusion
  4.6 0.0 copy-done
  4.6 1.4 reshape.34.pan
  6.0 138.2 %shard_map.77 = (f32[256,512]{1,0:T(8,128)}, f32[256,128]{1,0:T(8,128)}) custom-call(f32[2,512,512]{2,1,0:T(8,128)} %bitcast.6, f32[2,2,128,512]{3,2,1,0:T(8,128)} %reshape.34.pan, f32[2,2,128,128]{3,2,1,0:T(8,128)} %bitcast.7, f32[2,4]{1,0:T(2,128)} %copy-done, f32[1,2]{1,0:T(1,128)} %weight.1), custom_call_target="tpu_custom_call" | custom-call | flops 25999998976 | bytes 6000000 | tf_op jit(solution)/shard_map/pallas_call | solution.py:294
  144.2 1.9 %copy.15 = f32[256,512]{1,0:T(8,128)} copy(f32[256,512]{1,0:T(8,128)} %get-tuple-element.8) | data formatting | bytes 1048576
  146.1 1.6 %copy.16 = f32[2,128,128]{2,1,0:T(8,128)} copy(f32[2,128,128]{2,1,0:T(8,128)} %bitcast.5) | data formatting | bytes 262144
Async XLA Ops:
  2.1 2.5 %copy-start = (f32[2,4]{1,0:T(2,128)}, f32[2,4]{1,0:T(2,128)S(1)}, u32[]{:S(2)}) copy-start(f32[2,4]{1,0:T(2,128)S(1)} %multiply_reduce_fusion.mask) | copy-start | bytes 100

commit v2 on v0

v2 whole, which is shorter than its diff:
```python
import jax
import jax.numpy as jnp
from jax import lax
from jax.experimental import pallas as pl
from jax.experimental.pallas import tpu as pltpu
from jax.sharding import PartitionSpec as P

TILE = 128
NODES = 4
MESH = pl.DeviceIdType.MESH
HIGHEST = lax.Precision.HIGHEST
NT = (((1,), (1,)), ((), ()))
VMEM_LIMIT = 60 * 1024 * 1024
F32 = jnp.float32
PAN_ROWS = (slice(0, 192), slice(192, 256))
INV_ROWS = (slice(0, 384), slice(384, 512))
PAN_GROUPS = ((0, 1, 2), (3,))
INV_GROUPS = ((0, 1, 2), (3,))


def wrap(index):
    return lax.rem(index + 8, 4)


def dot(left, right, precision=None):
    return lax.dot_general(left, right, NT, precision=precision, preferred_element_type=F32)


def split(value):
    high = value.astype(jnp.bfloat16)
    return high, (value - high.astype(F32)).astype(jnp.bfloat16)


def kernel(
    inv, panel, diag, weight, node, pattern, dens, tiles,
    raw, pan, inv_all, pan_all, inv_split, pan_split, real_part, imag_part, tile_part,
    early, early_sum, early_other, late_rows, late_cols, tile_pieces, tile_sum, tile_rows, tile_out,
    send_sem, inv_recv, pan_recv, early_recv, other_recv, rows_recv, cols_recv, piece_recv,
    part_recv, gather_recv, out_recv, own_sem,
):
    p = lax.axis_index("pole")
    row = lax.axis_index("row")
    col = lax.axis_index("col")
    h, c = row // 2, row % 2
    y, l = col // 2, col % 2
    same = 1 - (c - l) * (c - l)

    def at(p_, h_, c_, y_, l_):
        return (p_, 2 * h_ + c_, 2 * y_ + l_)

    sibling = at(p, h, 1 - c, y, l)
    partner = at(p, h, c, y, 1 - l)
    up, down = at(p, h, c, wrap(y + 1), l), at(p, h, c, wrap(y - 1), l)
    on_right, on_left = at(p, wrap(h + 1), c, y, l), at(p, wrap(h - 1), c, y, l)
    others = [(wrap(h + d), k) for d in (1, 2, 3) for k in (0, 1)] + [(h, 1 - c)]
    reducers = [(wrap(p + d), (l + e) % 2) for d in range(4) for e in range(2)][1:]
    poles = [wrap(p + d) for d in (1, 2, 3)]

    raw_copy = pltpu.make_async_copy(panel.at[0], raw, own_sem.at[1])
    raw_copy.start()
    own_inv = pltpu.make_async_copy(inv.at[0], inv_all.at[y], own_sem.at[0])
    own_inv.start()

    barrier = pltpu.get_barrier_semaphore()
    greeted = [up, down] + [at(p, h_, c_, y, l) for h_, c_ in others]
    greeted += [at(p, wrap(h + l), k, y, 1 - l) for k in (0, 1)]
    greeted += [at(p, wrap(h - 1 + l), k, y, 1 - l) for k in (0, 1)]
    greeted += [at(p_, h, c, y, k) for p_ in poles for k in (0, 1)]
    for device in greeted:
        pl.semaphore_signal(barrier, inc=1, device_id=device, device_id_type=MESH)
    pl.semaphore_wait(barrier, len(greeted))

    slots = [0]
    waits = []

    def remote(source, target, recv, device, slot):
        return pltpu.make_async_remote_copy(
            src_ref=source, dst_ref=target, send_sem=send_sem.at[slot], recv_sem=recv,
            device_id=device, device_id_type=MESH,
        )

    def fresh():
        slots[0] += 1
        return slots[0] - 1

    def send(source, target, recv, device):
        copy = remote(source, target, recv, device, fresh())
        copy.start()
        waits.append((None, copy.wait_send))

    def send_if(flag, jobs):
        kept = [(job, fresh()) for job in jobs]

        @pl.when(flag)
        def _():
            for job, slot in kept:
                remote(*job, slot).start()

        def finish():
            for job, slot in kept:
                remote(*job, slot).wait_send()

        waits.append((flag, finish))

    def arrived(target, recv):
        remote(target, target, recv, sibling, 0).wait_recv()

    def entry(block, j):
        value = jnp.int32(0)
        for n in range(NODES):
            value += jnp.where(node[block] == n, pattern[n, j], 0)
        return value.astype(F32)

    mask = [[entry(block, j) for j in range(4)] for block in range(2)]

    def inv_at(k, ri, part):
        return inv_all.at[k, ri, INV_ROWS[part], :], inv_recv.at[k, ri, part]

    def send_inv(part, ri, device):
        send(inv.at[0, ri, INV_ROWS[part], :], *inv_at(y, ri, part), device)

    def pass_inv(part, k, ri, device):
        target, recv = inv_at(k, ri, part)
        send(target, target, recv, device)

    def arrived_inv(part, k, ri):
        arrived(*inv_at(k, ri, part))

    def pan_at(slot, ri, part):
        return pan_all.at[slot, ri, PAN_ROWS[part], :], pan_recv.at[slot, ri, part]

    own_slot = 2 * h + l
    cross_left = 2 * wrap(h - 1 + l) + 1 - l
    cross_right = 2 * wrap(h + l) + 1 - l
    same_left = 2 * wrap(h - 1) + l
    same_right = 2 * wrap(h + 1) + l
    far_left = 2 * wrap(h - 2 + l) + 1 - l
    far_right = 2 * wrap(h + 1 + l) + 1 - l
    same_far = 2 * wrap(h + 2) + l
    behind = 2 * l - 1

    def send_pan(part):
        def job(ri, device):
            return (pan.at[ri, PAN_ROWS[part], :], *pan_at(own_slot, ri, part), device)

        send_if(same == 0, [
            job(ri, at(p, wrap(h + way + l), ri, y, 1 - l)) for ri in (0, 1) for way in (0, -1)
        ])
        crossed = [
            (pan.at[ri, PAN_ROWS[part], :], *pan_at(8, ri, part), partner) for ri in (0, 1)
        ]
        away = [job(ri, at(p, wrap(h + behind), ri, y, l)) for ri in (0, 1)]
        shared = [job(ri, sibling) for ri in (0, 1)]
        send_if(same == 1, crossed + away + shared)

        @pl.when(same == 1)
        def _():
            for ri in (0, 1):
                target, recv = pan_at(own_slot, ri, part)
                pltpu.make_async_copy(pan.at[ri, PAN_ROWS[part], :], target, recv).start()

    def pass_pan(part, slot, device):
        target, recv = pan_at(slot, c, part)
        send(target, target, recv, device)

    def arrived_pan(part, slot, ri):
        arrived(*pan_at(slot, ri, part))

    def pass_on(part):
        @pl.when(same == 0)
        def _():
            for ri in (0, 1):
                arrived_pan(part, 8, ri)

        send_if(same == 0, [
            (pan_at(8, ri, part)[0], *pan_at(2 * h + 1 - l, ri, part), at(p, wrap(h + behind), ri, y, 1 - l))
            for ri in (0, 1)
        ])
        arrived_pan(part, cross_left, c)
        pass_pan(part, cross_left, on_right)
        pass_pan(part, cross_left, sibling)
        arrived_pan(part, cross_right, c)
        pass_pan(part, cross_right, on_left)
        pass_pan(part, cross_right, sibling)
        arrived_inv(part, wrap(y - 1), 0)
        pass_inv(part, wrap(y - 1), 0, up)
        arrived_inv(part, wrap(y + 1), 1)
        pass_inv(part, wrap(y + 1), 1, down)
        arrived_pan(part, same_left, c)
        arrived_pan(part, same_right, c)
        pass_pan(part, (1 - c) * same_left + c * same_right, at(p, wrap(h + 1 - 2 * c), c, y, l))
        pass_pan(part, same_left, sibling)
        pass_pan(part, same_right, sibling)

    def split_inv(part, k):
        columns = pl.ds(pl.multiple_of(k * 512, 512), 512)
        for g in INV_GROUPS[part]:
            for ri in (0, 1):
                high, low = split(inv_all[k, ri, g * TILE:(g + 1) * TILE, :])
                inv_split[0, g, ri * TILE:(ri + 1) * TILE, columns] = high
                inv_split[1, g, ri * TILE:(ri + 1) * TILE, columns] = low

    def split_pan(part, slot):
        columns = pl.ds(pl.multiple_of((slot // 2) * 512, 512), 512)
        for g in PAN_GROUPS[part]:
            for ri in (0, 1):
                high, low = split(pan_all[slot, ri, g * 64:(g + 1) * 64, :])
                begin = ri * TILE + (slot % 2) * 64
                pan_split[g, pl.ds(pl.multiple_of(begin, 64), 64), columns] = high
                pan_split[g, pl.ds(pl.multiple_of(begin + 256, 64), 64), columns] = low

    def near(part):
        for slot in (own_slot,):
            arrived_pan(part, slot, 0)
            arrived_pan(part, slot, 1)
            split_pan(part, slot)
        for slot in (cross_left, cross_right, same_left, same_right):
            arrived_pan(part, slot, 1 - c)
            split_pan(part, slot)
        arrived_inv(part, wrap(y - 1), 1)
        split_inv(part, wrap(y - 1))
        arrived_inv(part, wrap(y + 1), 0)
        split_inv(part, wrap(y + 1))

    def far(part):
        for slot in (far_left, far_right, same_far):
            arrived_pan(part, slot, c)
            pass_pan(part, slot, sibling)
        k = wrap(y + 2)
        arrived_inv(part, k, 0)
        arrived_inv(part, k, 1)
        split_inv(part, k)
        for slot in (far_left, far_right, same_far):
            arrived_pan(part, slot, 1 - c)
            split_pan(part, slot)

    real_weight = weight[0, 0]
    imag_weight = weight[0, 1]

    def multiply(g, block):
        both = dot(pan_split[g], inv_split[0, block])
        rest = dot(pan_split[g, 0:256, :], inv_split[1, block])
        from_real = both[0:TILE] + both[256:384] + rest[0:TILE]
        from_imag = both[TILE:256] + both[384:512] + rest[TILE:256]
        real = from_real[:, 0:TILE] - from_imag[:, TILE:256]
        imag = from_imag[:, 0:TILE] + from_real[:, TILE:256]
        weighted_real = real_weight * real - imag_weight * imag
        weighted_imag = real_weight * imag + imag_weight * real
        rows = pl.ds(pl.multiple_of(g * 64, 64), 64)
        columns = pl.ds(pl.multiple_of(block * TILE, TILE), TILE)
        for k in (0, 1):
            real_part[k, rows, columns] = weighted_real[k * 64:(k + 1) * 64]
            imag_part[k, rows, columns] = weighted_imag[k * 64:(k + 1) * 64]

    def loop(begin, end, body):
        def step(i, _):
            body(i)
            return 0

        lax.fori_loop(begin, end, step, 0)

    def multiply_early(i):
        multiply(i // 3, i % 3)

    send_inv(0, 0, up)
    send_inv(0, 1, down)
    send_inv(0, 1, up)
    send_inv(0, 0, down)
    raw_copy.wait()
    for part in (0, 1):
        for g in PAN_GROUPS[part]:
            rows = slice(g * 64, (g + 1) * 64)
            for ri in (0, 1):
                value = raw[rows, ri, :]
                for j in range(4):
                    columns = slice(j * TILE, (j + 1) * TILE)
                    pan[ri, rows, columns] = value[:, columns] * mask[g // 2][j]
        if part == 0:
            send_pan(0)
    own_inv.wait()
    split_inv(0, y)
    split_inv(1, y)
    pass_on(0)
    send_inv(1, 0, up)
    send_inv(1, 1, down)
    send_pan(1)
    send_inv(1, 1, up)
    send_inv(1, 0, down)
    near(0)
    far(0)

    loop(0, 4, multiply_early)
    pass_on(1)
    loop(4, 9, multiply_early)

    rows_first = pl.ds(pl.multiple_of(p * 48, 16), 48)
    rows_last = pl.ds(pl.multiple_of(192 + p * 16, 16), 16)

    def first_of(p_):
        return pl.ds(pl.multiple_of(p_ * 48, 16), 48)

    def last_of(p_):
        return pl.ds(pl.multiple_of(192 + p_ * 16, 16), 16)

    for p_ in poles:
        send(real_part.at[:, first_of(p_), 0:384], early.at[p], early_recv.at[p], at(p_, h, c, y, l))
    near(1)
    early_sum[...] = real_part[:, rows_first, 0:384]
    for p_ in poles:
        arrived(early.at[p_], early_recv.at[p_])
        early_sum[...] += early[p_]
    send(early_sum.at[1 - l], early_other, other_recv, partner)
    far(1)
    arrived(early_other, other_recv)

    def masked(total, begin, columns):
        upper = begin // TILE
        for j in columns:
            wide = slice((j - columns[0]) * TILE, (j - columns[0] + 1) * TILE)
            factor = jnp.where(upper == 0, mask[0][j], mask[1][j])
            dens[pl.ds(pl.multiple_of(begin, 16), 16), j * TILE:(j + 1) * TILE] = -factor * total[:, wide]

    for s in range(3):
        inner = slice(s * 16, (s + 1) * 16)
        masked(early_sum[l, inner, :] + early_other[inner, :], p * 48 + s * 16, (0, 1, 2))
    for p_ in poles:
        send(dens.at[rows_first, 0:384], dens.at[rows_first, 0:384], out_recv.at[p, 0], at(p_, h, c, y, l))

    me = 2 * p + l
    loop(0, 4, lambda i: multiply(3, i))
    for p_, l_ in reducers:
        send(real_part.at[l_, last_of(p_), :], late_rows.at[me], rows_recv.at[me], at(p_, h, c, y, l_))
    loop(0, 3, lambda i: multiply(i, 3))
    for p_, l_ in reducers:
        send(real_part.at[l_, first_of(p_), 384:512], late_cols.at[me], cols_recv.at[me], at(p_, h, c, y, l_))

    other = same * (2 * h + 1 - l) + (1 - same) * 8
    here = ((7 - row) // 7).astype(F32)
    for o in (0, 1):
        for half in (0, 1):
            inner = slice(half * TILE, (half + 1) * TILE)
            k = l if o == 0 else 1 - l
            left = (pan, pan_all.at[other])[o]
            tile = dot(left[0, inner, :], real_part[k, inner, :], HIGHEST)
            tile -= dot(left[1, inner, :], imag_part[k, inner, :], HIGHEST)
            if o == 0:
                tile += here * (real_weight * diag[0, half, 0] - imag_weight * diag[0, half, 1])
            tile_part[k, inner, :] = tile

    def quarter(p_):
        return pl.ds(pl.multiple_of(p_ * 64, 64), 64)

    for p_, l_ in reducers:
        send(tile_part.at[l_, quarter(p_), :], tile_pieces.at[me], piece_recv.at[me], at(p_, h, c, y, l_))

    def collect(own, buffer, recv):
        total = own
        for p_, l_ in reducers:
            k = 2 * p_ + l_
            arrived(buffer.at[k], recv.at[k])
            total += buffer[k]
        return total

    masked(collect(real_part[l, rows_last, :], late_rows, rows_recv), 192 + p * 16, (0, 1, 2, 3))
    for p_ in poles:
        send(dens.at[rows_last, :], dens.at[rows_last, :], out_recv.at[p, 1], at(p_, h, c, y, l))
    total = collect(real_part[l, rows_first, 384:512], late_cols, cols_recv)
    for s in range(3):
        masked(total[s * 16:(s + 1) * 16], p * 48 + s * 16, (3,))
    for p_ in poles:
        send(dens.at[rows_first, 384:512], dens.at[rows_first, 384:512], out_recv.at[p, 2], at(p_, h, c, y, l))

    tile_sum[...] = collect(tile_part[l, quarter(p), :], tile_pieces, piece_recv)

    def eighth(k):
        return pl.ds(pl.multiple_of(k * 8, 8), 8)

    for h_, c_ in others:
        send(tile_sum.at[eighth(2 * h_ + c_), :], tile_rows.at[row], part_recv.at[row], at(p, h_, c_, y, l))
    total = tile_sum[eighth(row), :]
    for h_, c_ in others:
        k = 2 * h_ + c_
        arrived(tile_rows.at[k], part_recv.at[k])
        total += tile_rows[k]
    tile_out[eighth(row), :] = total
    for h_, c_ in others:
        send(tile_out.at[eighth(row), :], tile_out.at[eighth(row), :], gather_recv.at[row], at(p, h_, c_, y, l))
    for h_, c_ in others:
        k = 2 * h_ + c_
        arrived(tile_out.at[eighth(k), :], gather_recv.at[k])
    tiles[quarter(p), :] = tile_out[...]
    for p_ in poles:
        send(tiles.at[quarter(p), :], tiles.at[quarter(p), :], out_recv.at[p, 3], at(p_, h, c, y, l))
    for p_ in poles:
        for k, target in enumerate((
            dens.at[first_of(p_), 0:384], dens.at[last_of(p_), :], dens.at[first_of(p_), 384:512],
            tiles.at[quarter(p_), :],
        )):
            arrived(target, out_recv.at[p_, k])

    for flag, finish in waits:
        if flag is None:
            finish()
        else:
            pl.when(flag)(finish)


def shards(root_inverse, panel, diag_inverse, pole_weight, block_node, pattern):
    dma = pltpu.SemaphoreType.DMA
    vmem = pl.BlockSpec(memory_space=pltpu.VMEM)
    smem = pl.BlockSpec(memory_space=pltpu.SMEM)
    hbm = pl.BlockSpec(memory_space=pl.ANY)
    half = jnp.bfloat16
    dens, tiles = pl.pallas_call(
        kernel,
        out_shape=(jax.ShapeDtypeStruct((256, 512), F32), jax.ShapeDtypeStruct((256, TILE), F32)),
        in_specs=[hbm, hbm, vmem, smem, smem, smem],
        out_specs=(vmem, vmem),
        scratch_shapes=[
            pltpu.VMEM((256, 2, 512), F32),
            pltpu.VMEM((2, 256, 512), F32),
            pltpu.VMEM((4, 2, 512, 512), F32),
            pltpu.VMEM((9, 2, 256, 512), F32),
            pltpu.VMEM((2, 4, 256, 2048), half),
            pltpu.VMEM((4, 512, 2048), half),
            pltpu.VMEM((2, 256, 512), F32),
            pltpu.VMEM((2, 256, 512), F32),
            pltpu.VMEM((2, 256, TILE), F32),
            pltpu.VMEM((4, 2, 48, 384), F32),
            pltpu.VMEM((2, 48, 384), F32),
            pltpu.VMEM((48, 384), F32),
            pltpu.VMEM((8, 16, 512), F32),
            pltpu.VMEM((8, 48, TILE), F32),
            pltpu.VMEM((8, 64, TILE), F32),
            pltpu.VMEM((64, TILE), F32),
            pltpu.VMEM((8, 8, TILE), F32),
            pltpu.VMEM((64, TILE), F32),
            dma((128,)),
            dma((4, 2, 2)), dma((9, 2, 2)),
            dma((4,)), dma, dma((8,)), dma((8,)), dma((8,)),
            dma((8,)), dma((8,)), dma((4, 4)), dma((2,)),
        ],
        compiler_params=pltpu.CompilerParams(
            collective_id=0, has_side_effects=True, vmem_limit_bytes=VMEM_LIMIT
        ),
        cost_estimate=pl.CostEstimate(flops=26_000_000_000, bytes_accessed=6_000_000, transcendentals=0),
    )(root_inverse, panel, diag_inverse, pole_weight, block_node, pattern)
    return dens, tiles.reshape(2, TILE, TILE)


def solution(mesh):
    placed = (
        P("pole", None, "row", "col"),
        P("pole", "col", None, "row"),
        P("pole", "col", None, None, None),
        P("pole", None),
        P("col"),
        P(None, "row"),
    )
    return jax.shard_map(
        shards,
        mesh=mesh,
        in_specs=placed,
        out_specs=(P("col", "row"), P("col", None, None)),
        check_vma=False,
    )
```

time: 618 us -> 143 us (0.23)
  waiting for transfers between devices: 531 us -> 0 us
  Pallas kernels: 0 us -> 139 us
  matrix products: 48.7 us -> 0 us
  local copies, waits for them, and re-layouts: 17.1 us -> 3.44 us
  between operations: 13.9 us -> 0.64 us
    all_gather x2 -> x0, waiting for transfers between devices: 411 us -> none  [the longest x1 315 us: shards(): portion = lax.all_gather(root_inverse, 'col', axis=3, tiled=True)]
    pallas_call x0 -> x1, Pallas kernels: none -> 139 us  [shards(): pl.pallas_call(kernel, out_shape=(jax.ShapeDtypeStruct((256, 512), F32),...]
    psum x2 -> x0, waiting for transfers between devices: 119 us -> none  [the longest x1 73 us: shards(): summed_real, summed_imag = lax.psum((coupling_real, coupling_imag), 'row')]
    dot_general x9 -> x0, matrix products: 48.7 us -> none  [the longest x4 44 us: contract(): lax.dot_general(left, right, dims, precision=lax.Precision.HIGHEST, prefe...]
    slice x2 -> x0, local copies, waits for them, and re-layouts: 12.9 us -> none  [the longest x1 12.3 us: shards(): gathered[:, 0]]
  transfers between devices with their start and end apart: 4 -> 0, of which waited for: 4 -> 0; matrix products, arithmetic and copies ran while one was open for 2% -> 0% of each run, Pallas kernels for 0% -> 0%
where the time goes in v2:
time: 143 us
  Pallas kernels  139 us (97%)
  local copies, waits for them, and re-layouts  3.44 us (2%)
    pallas_call x1, Pallas kernels, shards(): pl.pallas_call(kernel, out_shape=(jax.ShapeDtypeStruct((256, 512), F32),...  139 us
    unnamed x2, local copies, waits for them, and re-layouts  3.44 us

profile of v2, /device:TPU:1, one launch (start us, length us, event | category | flops | bytes accessed | tf_op | source)
XLA Modules:
  0.0 142.7 jit_solution(2138404304320702069)
XLA Ops:
  0.6 138.6 %shard_map.77 = (f32[256,512]{1,0:T(8,128)}, f32[256,128]{1,0:T(8,128)}) custom-call(f32[1,2,512,512]{3,2,1,0:T(8,128)} %inv.1, f32[1,256,2,512]{3,2,1,0:T(2,128)} %panel.1, f32[1,2,2,128,128]{4,3,2,1,0:T(8,128)} %diag.1, f32[1,2]{1,0:T(1,128)} %weight.1, s32[2]{0:T(128)} %node.1, s32[4,4]{1,0:T(4,128)} %pattern.1), custom_call_target="tpu_custom_call" | custom-call | flops 25999998976 | bytes 6000000 | tf_op jit(solution)/shard_map/pallas_call | solution.py:414
  139.3 1.9 %copy.10 = f32[256,512]{1,0:T(8,128)} copy(f32[256,512]{1,0:T(8,128)} %get-tuple-element.8) | data formatting | bytes 1048576
  141.1 1.6 %copy.11 = f32[2,128,128]{2,1,0:T(8,128)} copy(f32[2,128,128]{2,1,0:T(8,128)} %bitcast.1) | data formatting | bytes 262144

commit v3 on v2

v3 whole, which is shorter than its diff:
```python
import jax
import jax.numpy as jnp
from jax import lax
from jax.experimental import pallas as pl
from jax.experimental.pallas import tpu as pltpu
from jax.sharding import PartitionSpec as P

TILE = 128
NODES = 4
MESH = pl.DeviceIdType.MESH
HIGHEST = lax.Precision.HIGHEST
NT = (((1,), (1,)), ((), ()))
VMEM_LIMIT = 60 * 1024 * 1024
F32 = jnp.float32
PARTS = 4
SENDS = 320


def wrap(index):
    return lax.rem(index + 8, 4)


def dot(left, right, precision=None):
    return lax.dot_general(left, right, NT, precision=precision, preferred_element_type=F32)


def split(value):
    high = value.astype(jnp.bfloat16)
    return high, (value - high.astype(F32)).astype(jnp.bfloat16)


def kernel(
    inv, panel, diag, weight, node, pattern, dens, tiles,
    raw, pan, inv_all, pan_all, inv_split, pan_split, begun, real_part, left_split, right_split, tile_part,
    early, early_sum, early_other, late_rows, late_cols, tile_other, tile_sum, tile_pieces, tile_rows,
    send_sem, inv_recv, pan_recv, early_recv, other_recv, rows_recv, cols_recv, core_recv, piece_recv,
    part_recv, out_recv, tile_recv, own_sem,
):
    p = lax.axis_index("pole")
    row = lax.axis_index("row")
    col = lax.axis_index("col")
    h, c = row // 2, row % 2
    y, l = col // 2, col % 2
    same = 1 - (c - l) * (c - l)

    def at(p_, h_, c_, y_, l_):
        return (p_, 2 * h_ + c_, 2 * y_ + l_)

    sibling = at(p, h, 1 - c, y, l)
    partner = at(p, h, c, y, 1 - l)
    up, down = at(p, h, c, wrap(y + 1), l), at(p, h, c, wrap(y - 1), l)
    on_right, on_left = at(p, wrap(h + 1), c, y, l), at(p, wrap(h - 1), c, y, l)
    others = [(wrap(h + d), k) for d in (1, 2, 3) for k in (0, 1)] + [(h, 1 - c)]
    heights = [wrap(h + d) for d in (1, 2, 3)]
    reducers = [(wrap(p + d), (l + e) % 2) for d in range(4) for e in range(2)][1:]
    poles = [wrap(p + d) for d in (1, 2, 3)]
    copies = [(p_, c_) for p_ in poles for c_ in (c, 1 - c)] + [(p, 1 - c)]

    raw_copy = pltpu.make_async_copy(panel.at[0], raw, own_sem.at[1])
    raw_copy.start()
    own_inv = pltpu.make_async_copy(inv.at[0], inv_all.at[y], own_sem.at[0])
    own_inv.start()

    barrier = pltpu.get_barrier_semaphore()
    greeted = [up, down] + [at(p, h_, c_, y, l) for h_, c_ in others]
    greeted += [at(p, wrap(h + l), k, y, 1 - l) for k in (0, 1)]
    greeted += [at(p, wrap(h - 1 + l), k, y, 1 - l) for k in (0, 1)]
    greeted += [at(p_, h, c, y, k) for p_ in poles for k in (0, 1)]
    greeted += [at(p_, h, 1 - c, y, l) for p_ in poles]
    for device in greeted:
        pl.semaphore_signal(barrier, inc=1, device_id=device, device_id_type=MESH)

    slots = [0]
    waits = []

    def remote(source, target, recv, device, slot):
        return pltpu.make_async_remote_copy(
            src_ref=source, dst_ref=target, send_sem=send_sem.at[slot], recv_sem=recv,
            device_id=device, device_id_type=MESH,
        )

    def fresh():
        slots[0] += 1
        return slots[0] - 1

    def send(source, target, recv, device):
        copy = remote(source, target, recv, device, fresh())
        copy.start()
        waits.append((None, copy.wait_send))

    def send_if(flag, jobs):
        kept = [(job, fresh()) for job in jobs]

        @pl.when(flag)
        def _():
            for job, slot in kept:
                remote(*job, slot).start()

        def finish():
            for job, slot in kept:
                remote(*job, slot).wait_send()

        waits.append((flag, finish))

    def arrived(target, recv):
        remote(target, target, recv, sibling, 0).wait_recv()

    def entry(block, j):
        value = jnp.int32(0)
        for n in range(NODES):
            value += jnp.where(node[block] == n, pattern[n, j], 0)
        return value.astype(F32)

    mask = [[entry(block, j) for j in range(4)] for block in range(2)]

    def inv_at(k, ri, part):
        return inv_all.at[k, ri, pl.ds(part * TILE, TILE), :], inv_recv.at[k, ri, part]

    def send_inv(part, ri, device):
        send(inv.at[0, ri, pl.ds(part * TILE, TILE), :], *inv_at(y, ri, part), device)

    def pass_inv(part, k, ri, device):
        target, recv = inv_at(k, ri, part)
        send(target, target, recv, device)

    def arrived_inv(part, k, ri):
        arrived(*inv_at(k, ri, part))

    def pan_at(slot, ri, part):
        return pan_all.at[slot, ri, pl.ds(part * 64, 64), :], pan_recv.at[slot, ri, part]

    own_slot = 2 * h + l
    cross_left = 2 * wrap(h - 1 + l) + 1 - l
    cross_right = 2 * wrap(h + l) + 1 - l
    same_left = 2 * wrap(h - 1) + l
    same_right = 2 * wrap(h + 1) + l
    far_left = 2 * wrap(h - 2 + l) + 1 - l
    far_right = 2 * wrap(h + 1 + l) + 1 - l
    same_far = 2 * wrap(h + 2) + l
    behind = 2 * l - 1

    def send_pan(part):
        def job(ri, device):
            return (pan.at[ri, pl.ds(part * 64, 64), :], *pan_at(own_slot, ri, part), device)

        send_if(same == 0, [
            job(ri, at(p, wrap(h + way + l), ri, y, 1 - l)) for ri in (0, 1) for way in (0, -1)
        ])
        crossed = [
            (pan.at[ri, pl.ds(part * 64, 64), :], *pan_at(8, ri, part), partner) for ri in (0, 1)
        ]
        away = [job(ri, at(p, wrap(h + behind), ri, y, l)) for ri in (0, 1)]
        shared = [job(ri, sibling) for ri in (0, 1)]
        send_if(same == 1, crossed + away + shared)

        @pl.when(same == 1)
        def _():
            for ri in (0, 1):
                target, recv = pan_at(own_slot, ri, part)
                pltpu.make_async_copy(pan.at[ri, pl.ds(part * 64, 64), :], target, recv).start()

    def pass_pan(part, slot, device):
        target, recv = pan_at(slot, c, part)
        send(target, target, recv, device)

    def arrived_pan(part, slot, ri):
        arrived(*pan_at(slot, ri, part))

    def pass_on(part):
        @pl.when(same == 0)
        def _():
            for ri in (0, 1):
                arrived_pan(part, 8, ri)

        send_if(same == 0, [
            (pan_at(8, ri, part)[0], *pan_at(2 * h + 1 - l, ri, part), at(p, wrap(h + behind), ri, y, 1 - l))
            for ri in (0, 1)
        ])
        arrived_pan(part, cross_left, c)
        pass_pan(part, cross_left, on_right)
        pass_pan(part, cross_left, sibling)
        arrived_pan(part, cross_right, c)
        pass_pan(part, cross_right, on_left)
        pass_pan(part, cross_right, sibling)
        arrived_inv(part, wrap(y - 1), 0)
        pass_inv(part, wrap(y - 1), 0, up)
        arrived_inv(part, wrap(y + 1), 1)
        pass_inv(part, wrap(y + 1), 1, down)

    def pass_same(part):
        arrived_pan(part, same_left, c)
        arrived_pan(part, same_right, c)
        pass_pan(part, (1 - c) * same_left + c * same_right, at(p, wrap(h + 1 - 2 * c), c, y, l))
        pass_pan(part, same_left, sibling)
        pass_pan(part, same_right, sibling)

    def direct(part):
        send_inv(part, 0, up)
        send_inv(part, 1, down)
        send_pan(part)
        send_inv(part, 1, up)
        send_inv(part, 0, down)

    def split_inv(part, k):
        columns = pl.ds(pl.multiple_of(k * 512, 512), 512)
        for ri in (0, 1):
            high, low = split(inv_all[k, ri, part * TILE:(part + 1) * TILE, :])
            inv_split[0, part, ri * TILE:(ri + 1) * TILE, columns] = high
            inv_split[1, part, ri * TILE:(ri + 1) * TILE, columns] = low

    def split_pan(part, slot):
        columns = pl.ds(pl.multiple_of((slot // 2) * 512, 512), 512)
        for ri in (0, 1):
            high, low = split(pan_all[slot, ri, part * 64:(part + 1) * 64, :])
            begin = ri * TILE + (slot % 2) * 64
            pan_split[part, pl.ds(pl.multiple_of(begin, 64), 64), columns] = high
            pan_split[part, pl.ds(pl.multiple_of(begin + 256, 64), 64), columns] = low

    def split_left(part, k, source):
        rows = slice(part * 64, (part + 1) * 64)
        for ri in (0, 1):
            value = source[ri, rows, :]
            high, low = split(-value if ri else value)
            left_split[k, part * 64:(part + 1) * 64, ri * 512:(ri + 1) * 512] = high
            left_split[k, 256 + part * 64:256 + (part + 1) * 64, ri * 512:(ri + 1) * 512] = low

    other = same * (2 * h + 1 - l) + (1 - same) * 8

    def near(part):
        for ri in (0, 1):
            arrived_pan(part, own_slot, ri)
        split_pan(part, own_slot)
        for slot in (cross_left, cross_right, same_left, same_right):
            arrived_pan(part, slot, 1 - c)
            split_pan(part, slot)
        split_left(part, 1 - l, pan_all.at[other])
        arrived_inv(part, wrap(y - 1), 1)
        split_inv(part, wrap(y - 1))
        arrived_inv(part, wrap(y + 1), 0)
        split_inv(part, wrap(y + 1))

    def far(part):
        for slot in (far_left, far_right, same_far):
            arrived_pan(part, slot, c)
            pass_pan(part, slot, sibling)
        k = wrap(y + 2)
        arrived_inv(part, k, 0)
        arrived_inv(part, k, 1)
        split_inv(part, k)
        for slot in (far_left, far_right, same_far):
            arrived_pan(part, slot, 1 - c)
            split_pan(part, slot)

    real_weight = weight[0, 0]
    imag_weight = weight[0, 1]

    def sums(g, block, ks):
        from_real, from_imag = 0.0, 0.0
        for k in ks:
            columns = slice(None) if k is None else pl.ds(pl.multiple_of(k * 512, 512), 512)
            both = dot(pan_split[g, :, columns], inv_split[0, block, :, columns])
            rest = dot(pan_split[g, 0:256, columns], inv_split[1, block, :, columns])
            from_real += both[0:TILE] + both[256:384] + rest[0:TILE]
            from_imag += both[TILE:256] + both[384:512] + rest[TILE:256]
        return from_real, from_imag

    def finish(g, block, from_real, from_imag):
        real = from_real[:, 0:TILE] - from_imag[:, TILE:256]
        imag = from_imag[:, 0:TILE] + from_real[:, TILE:256]
        weighted_real = real_weight * real - imag_weight * imag
        weighted_imag = real_weight * imag + imag_weight * real
        rows = pl.ds(pl.multiple_of(g * 64, 64), 64)
        columns = pl.ds(pl.multiple_of(block * TILE, TILE), TILE)
        beside = pl.ds(pl.multiple_of(512 + block * TILE, TILE), TILE)
        for k in (0, 1):
            inner = slice(k * 64, (k + 1) * 64)
            real_part[k, rows, columns] = weighted_real[inner]
            for place, value in ((columns, weighted_real[inner]), (beside, weighted_imag[inner])):
                high, low = split(value)
                right_split[k, 0, rows, place] = high
                right_split[k, 1, rows, place] = low

    def multiply(g, block):
        finish(g, block, *sums(g, block, (None,)))

    def begin_block(place, g, block, ks):
        from_real, from_imag = sums(g, block, ks)
        begun[place, 0] = from_real
        begun[place, 1] = from_imag

    def end_block(place, g, block, ks):
        from_real, from_imag = sums(g, block, ks)
        finish(g, block, begun[place, 0] + from_real, begun[place, 1] + from_imag)

    def loop(begin, end, body):
        def step(i, _):
            body(i)
            return 0

        lax.fori_loop(begin, end, step, 0)

    def corner(part):
        loop(0, part + 1, lambda i: multiply(part, i))
        if part:
            loop(0, part, lambda i: multiply(i, part))

    raw_copy.wait()
    for g in range(PARTS):
        rows = slice(g * 64, (g + 1) * 64)
        for ri in (0, 1):
            value = raw[rows, ri, :]
            for j in range(4):
                columns = slice(j * TILE, (j + 1) * TILE)
                pan[ri, rows, columns] = value[:, columns] * mask[g // 2][j]
    pl.semaphore_wait(barrier, len(greeted))
    direct(0)
    direct(1)
    own_inv.wait()
    for part in range(PARTS):
        split_inv(part, y)
        split_left(part, l, pan)
    pass_on(0)
    direct(2)
    pass_on(1)
    pass_same(0)
    direct(3)
    pass_on(2)
    pass_same(1)
    near(0)
    far(0)
    corner(0)
    pass_on(3)
    pass_same(2)
    near(1)
    far(1)
    corner(1)
    near(2)
    far(2)
    corner(2)

    rows_first = pl.ds(pl.multiple_of(p * 48, 16), 48)
    rows_last = pl.ds(pl.multiple_of(192 + p * 16, 16), 16)

    def first_of(p_):
        return pl.ds(pl.multiple_of(p_ * 48, 16), 48)

    def last_of(p_):
        return pl.ds(pl.multiple_of(192 + p_ * 16, 16), 16)

    for p_ in poles:
        send(real_part.at[:, first_of(p_), 0:384], early.at[p], early_recv.at[p], at(p_, h, c, y, l))
    pass_same(3)
    near(3)
    there, missing = [wrap(h - 1 + l), wrap(h + l)], [wrap(h + 1 + l), wrap(h + 2 + l)]
    loop(0, 3, lambda i: begin_block(i, 3, i, there))
    loop(0, 3, lambda i: begin_block(3 + i, i, 3, [wrap(y - 1), y, wrap(y + 1)]))
    early_sum[...] = real_part[:, rows_first, 0:384]
    for p_ in poles:
        arrived(early.at[p_], early_recv.at[p_])
        early_sum[...] += early[p_]
    send(early_sum.at[1 - l], early_other, other_recv, partner)
    far(3)
    loop(0, 3, lambda i: end_block(i, 3, i, missing))
    loop(0, 3, lambda i: end_block(3 + i, i, 3, [wrap(y + 2)]))
    multiply(3, 3)

    here = ((7 - row) // 7).astype(F32)
    for o in (0, 1):
        k = l if o == 0 else 1 - l
        both = dot(left_split[k], right_split[k, 0])
        both = both[0:256] + both[256:512] + dot(left_split[k, 0:256, :], right_split[k, 1])
        for half in (0, 1):
            inner = slice(half * TILE, (half + 1) * TILE)
            tile = both[inner, inner]
            if o == 0:
                tile += here * (real_weight * diag[0, half, 0] - imag_weight * diag[0, half, 1])
            tile_part[k, half] = tile
    send(tile_part.at[:, 1 - c], tile_other, core_recv, sibling)

    me = 2 * p + l
    for p_, l_ in reducers:
        send(real_part.at[l_, last_of(p_), :], late_rows.at[me], rows_recv.at[me], at(p_, h, c, y, l_))
        send(real_part.at[l_, first_of(p_), 384:512], late_cols.at[me], cols_recv.at[me], at(p_, h, c, y, l_))

    def piece(p_):
        return pl.ds(pl.multiple_of(p_ * 32, 32), 32)

    def collect(own, buffer, recv):
        total = own
        for p_, l_ in reducers:
            k = 2 * p_ + l_
            arrived(buffer.at[k], recv.at[k])
            total += buffer[k]
        return total

    arrived(tile_other, core_recv)
    tile_sum[...] = tile_part[:, c] + tile_other[...]
    for p_, l_ in reducers:
        send(tile_sum.at[l_, piece(p_), :], tile_pieces.at[me], piece_recv.at[me], at(p_, h, c, y, l_))
    arrived(early_other, other_recv)

    def masked(total, begin, columns):
        upper = begin // TILE
        for j in columns:
            wide = slice((j - columns[0]) * TILE, (j - columns[0] + 1) * TILE)
            factor = jnp.where(upper == 0, mask[0][j], mask[1][j])
            dens[pl.ds(pl.multiple_of(begin, 16), 16), j * TILE:(j + 1) * TILE] = -factor * total[:, wide]

    for s in range(3):
        inner = slice(s * 16, (s + 1) * 16)
        masked(early_sum[l, inner, :] + early_other[inner, :], p * 48 + s * 16, (0, 1, 2))
    for p_ in poles:
        send(dens.at[rows_first, 0:384], dens.at[rows_first, 0:384], out_recv.at[p, 0], at(p_, h, c, y, l))

    tile_rows[h] = collect(tile_sum[l, piece(p), :], tile_pieces, piece_recv)
    for h_ in heights:
        send(tile_rows.at[h], tile_rows.at[h], part_recv.at[h], at(p, h_, c, y, l))
    masked(collect(real_part[l, rows_last, :], late_rows, rows_recv), 192 + p * 16, (0, 1, 2, 3))
    for p_ in poles:
        send(dens.at[rows_last, :], dens.at[rows_last, :], out_recv.at[p, 1], at(p_, h, c, y, l))
    total = collect(real_part[l, rows_first, 384:512], late_cols, cols_recv)
    for s in range(3):
        masked(total[s * 16:(s + 1) * 16], p * 48 + s * 16, (3,))
    for p_ in poles:
        send(dens.at[rows_first, 384:512], dens.at[rows_first, 384:512], out_recv.at[p, 2], at(p_, h, c, y, l))
    for h_ in heights:
        arrived(tile_rows.at[h_], part_recv.at[h_])

    def tile_of(p_, c_):
        return tiles.at[pl.ds(pl.multiple_of(c_ * TILE + p_ * 32, 32), 32), :], tile_recv.at[2 * p_ + c_]

    mine, recv = tile_of(p, c)
    mine[...] = tile_rows[0] + tile_rows[1] + tile_rows[2] + tile_rows[3]
    for p_, c_ in copies:
        send(mine, mine, recv, at(p_, h, c_, y, l))
    for p_ in poles:
        for k, target in enumerate((
            dens.at[first_of(p_), 0:384], dens.at[last_of(p_), :], dens.at[first_of(p_), 384:512],
        )):
            arrived(target, out_recv.at[p_, k])
    for p_, c_ in copies:
        arrived(*tile_of(p_, c_))
    assert slots[0] <= SENDS

    for flag, finish in waits:
        if flag is None:
            finish()
        else:
            pl.when(flag)(finish)


def shards(root_inverse, panel, diag_inverse, pole_weight, block_node, pattern):
    dma = pltpu.SemaphoreType.DMA
    vmem = pl.BlockSpec(memory_space=pltpu.VMEM)
    smem = pl.BlockSpec(memory_space=pltpu.SMEM)
    hbm = pl.BlockSpec(memory_space=pl.ANY)
    half = jnp.bfloat16
    dens, tiles = pl.pallas_call(
        kernel,
        out_shape=(jax.ShapeDtypeStruct((256, 512), F32), jax.ShapeDtypeStruct((256, TILE), F32)),
        in_specs=[hbm, hbm, vmem, smem, smem, smem],
        out_specs=(vmem, vmem),
        scratch_shapes=[
            pltpu.VMEM((256, 2, 512), F32),
            pltpu.VMEM((2, 256, 512), F32),
            pltpu.VMEM((4, 2, 512, 512), F32),
            pltpu.VMEM((9, 2, 256, 512), F32),
            pltpu.VMEM((2, 4, 256, 2048), half),
            pltpu.VMEM((4, 512, 2048), half),
            pltpu.VMEM((6, 2, TILE, 256), F32),
            pltpu.VMEM((2, 256, 512), F32),
            pltpu.VMEM((2, 512, 1024), half),
            pltpu.VMEM((2, 2, 256, 1024), half),
            pltpu.VMEM((2, 2, TILE, TILE), F32),
            pltpu.VMEM((4, 2, 48, 384), F32),
            pltpu.VMEM((2, 48, 384), F32),
            pltpu.VMEM((48, 384), F32),
            pltpu.VMEM((8, 16, 512), F32),
            pltpu.VMEM((8, 48, TILE), F32),
            pltpu.VMEM((2, TILE, TILE), F32),
            pltpu.VMEM((2, TILE, TILE), F32),
            pltpu.VMEM((8, 32, TILE), F32),
            pltpu.VMEM((4, 32, TILE), F32),
            dma((SENDS,)),
            dma((4, 2, PARTS)), dma((9, 2, PARTS)),
            dma((4,)), dma, dma((8,)), dma((8,)), dma, dma((8,)),
            dma((4,)), dma((4, 3)), dma((8,)), dma((2,)),
        ],
        compiler_params=pltpu.CompilerParams(
            collective_id=0, has_side_effects=True, vmem_limit_bytes=VMEM_LIMIT
        ),
        cost_estimate=pl.CostEstimate(flops=26_000_000_000, bytes_accessed=6_000_000, transcendentals=0),
    )(root_inverse, panel, diag_inverse, pole_weight, block_node, pattern)
    return dens, tiles.reshape(2, TILE, TILE)


def solution(mesh):
    placed = (
        P("pole", None, "row", "col"),
        P("pole", "col", None, "row"),
        P("pole", "col", None, None, None),
        P("pole", None),
        P("col"),
        P(None, "row"),
    )
    return jax.shard_map(
        shards,
        mesh=mesh,
        in_specs=placed,
        out_specs=(P("col", "row"), P("col", None, None)),
        check_vma=False,
    )
```

time: 143 us -> 133 us (0.930)
  Pallas kernels: 139 us -> 128 us
    pallas_call x1, Pallas kernels: 139 us -> 128 us  [shards(): pl.pallas_call(kernel, out_shape=(jax.ShapeDtypeStruct((256, 512), F32),...]
where the time goes in v3:
time: 133 us; the launch traced here: 132 us
  Pallas kernels  128 us (96%)
  local copies, waits for them, and re-layouts  3.44 us (3%)
    pallas_call x1, Pallas kernels, shards(): pl.pallas_call(kernel, out_shape=(jax.ShapeDtypeStruct((256, 512), F32),...  128 us
    unnamed x2, local copies, waits for them, and re-layouts  3.44 us

profile of v3, /device:TPU:1, one launch (start us, length us, event | category | flops | bytes accessed | tf_op | source)
XLA Modules:
  0.0 132.4 jit_solution(14529122572449401796)
XLA Ops:
  0.6 128.3 %shard_map.77 = (f32[256,512]{1,0:T(8,128)}, f32[256,128]{1,0:T(8,128)}) custom-call(f32[1,2,512,512]{3,2,1,0:T(8,128)} %inv.1, f32[1,256,2,512]{3,2,1,0:T(2,128)} %panel.1, f32[1,2,2,128,128]{4,3,2,1,0:T(8,128)} %diag.1, f32[1,2]{1,0:T(1,128)} %weight.1, s32[2]{0:T(128)} %node.1, s32[4,4]{1,0:T(4,128)} %pattern.1), custom_call_target="tpu_custom_call" | custom-call | flops 25999998976 | bytes 6000000 | tf_op jit(solution)/shard_map/pallas_call | solution.py:458
  128.9 1.9 %copy.10 = f32[256,512]{1,0:T(8,128)} copy(f32[256,512]{1,0:T(8,128)} %get-tuple-element.8) | data formatting | bytes 1048576
  130.8 1.6 %copy.11 = f32[2,128,128]{2,1,0:T(8,128)} copy(f32[2,128,128]{2,1,0:T(8,128)} %bitcast.1) | data formatting | bytes 262144

commit v4 on v3

--- a/solution.py
+++ b/solution.py
@@ -31,9 +31,9 @@
 
 def kernel(
     inv, panel, diag, weight, node, pattern, dens, tiles,
-    raw, pan, inv_all, pan_all, inv_split, pan_split, begun, real_part, left_split, right_split, tile_part,
-    early, early_sum, early_other, late_rows, late_cols, tile_other, tile_sum, tile_pieces, tile_rows,
-    send_sem, inv_recv, pan_recv, early_recv, other_recv, rows_recv, cols_recv, core_recv, piece_recv,
+    raw, pan, inv_all, pan_all, inv_split, pan_split, real_part, left_split, right_split, tile_part,
+    early, early_sum, early_other, late_rows, tile_other, tile_sum, tile_pieces, tile_rows,
+    send_sem, inv_recv, pan_recv, early_recv, other_recv, rows_recv, core_recv, piece_recv,
     part_recv, out_recv, tile_recv, own_sem,
 ):
     p = lax.axis_index("pole")
@@ -101,6 +101,14 @@
                 remote(*job, slot).wait_send()
 
         waits.append((flag, finish))
+
+    def flush(count):
+        for flag, finish in waits[:count]:
+            if flag is None:
+                finish()
+            else:
+                pl.when(flag)(finish)
+        del waits[:count]
 
     def arrived(target, recv):
         remote(target, target, recv, sibling, 0).wait_recv()
@@ -182,6 +190,8 @@
         arrived_pan(part, cross_right, c)
         pass_pan(part, cross_right, on_left)
         pass_pan(part, cross_right, sibling)
+
+    def inv_on(part):
         arrived_inv(part, wrap(y - 1), 0)
         pass_inv(part, wrap(y - 1), 0, up)
         arrived_inv(part, wrap(y + 1), 1)
@@ -194,10 +204,9 @@
         pass_pan(part, same_left, sibling)
         pass_pan(part, same_right, sibling)
 
-    def direct(part):
+    def direct_inv(part):
         send_inv(part, 0, up)
         send_inv(part, 1, down)
-        send_pan(part)
         send_inv(part, 1, up)
         send_inv(part, 0, down)
 
@@ -234,35 +243,33 @@
             arrived_pan(part, slot, 1 - c)
             split_pan(part, slot)
         split_left(part, 1 - l, pan_all.at[other])
+
+    def far(part):
+        for slot in (far_left, far_right, same_far):
+            arrived_pan(part, slot, c)
+            pass_pan(part, slot, sibling)
+        for slot in (far_left, far_right, same_far):
+            arrived_pan(part, slot, 1 - c)
+            split_pan(part, slot)
+
+    def inv_done(part):
+        k = wrap(y + 2)
         arrived_inv(part, wrap(y - 1), 1)
         split_inv(part, wrap(y - 1))
         arrived_inv(part, wrap(y + 1), 0)
         split_inv(part, wrap(y + 1))
-
-    def far(part):
-        for slot in (far_left, far_right, same_far):
-            arrived_pan(part, slot, c)
-            pass_pan(part, slot, sibling)
-        k = wrap(y + 2)
         arrived_inv(part, k, 0)
         arrived_inv(part, k, 1)
         split_inv(part, k)
-        for slot in (far_left, far_right, same_far):
-            arrived_pan(part, slot, 1 - c)
-            split_pan(part, slot)
 
     real_weight = weight[0, 0]
     imag_weight = weight[0, 1]
 
-    def sums(g, block, ks):
-        from_real, from_imag = 0.0, 0.0
-        for k in ks:
-            columns = slice(None) if k is None else pl.ds(pl.multiple_of(k * 512, 512), 512)
-            both = dot(pan_split[g, :, columns], inv_split[0, block, :, columns])
-            rest = dot(pan_split[g, 0:256, columns], inv_split[1, block, :, columns])
-            from_real += both[0:TILE] + both[256:384] + rest[0:TILE]
-            from_imag += both[TILE:256] + both[384:512] + rest[TILE:256]
-        return from_real, from_imag
+    def join(both, rest):
+        return (
+            both[0:TILE] + both[256:384] + rest[0:TILE],
+            both[TILE:256] + both[384:512] + rest[TILE:256],
+        )
 
     def finish(g, block, from_real, from_imag):
         real = from_real[:, 0:TILE] - from_imag[:, TILE:256]
@@ -281,16 +288,23 @@
                 right_split[k, 1, rows, place] = low
 
     def multiply(g, block):
-        finish(g, block, *sums(g, block, (None,)))
-
-    def begin_block(place, g, block, ks):
-        from_real, from_imag = sums(g, block, ks)
-        begun[place, 0] = from_real
-        begun[place, 1] = from_imag
-
-    def end_block(place, g, block, ks):
-        from_real, from_imag = sums(g, block, ks)
-        finish(g, block, begun[place, 0] + from_real, begun[place, 1] + from_imag)
+        both = dot(pan_split[g], inv_split[0, block])
+        rest = dot(pan_split[g, 0:256, :], inv_split[1, block])
+        finish(g, block, *join(both, rest))
+
+    def multiply_wide(pair):
+        blocks = pl.ds(2 * pair, 2)
+        both = dot(pan_split[3], inv_split[0, blocks].reshape(512, 2048))
+        rest = dot(pan_split[3, 0:256, :], inv_split[1, blocks].reshape(512, 2048))
+        for k in (0, 1):
+            columns = slice(k * 256, (k + 1) * 256)
+            finish(3, 2 * pair + k, *join(both[:, columns], rest[:, columns]))
+
+    def multiply_tall():
+        both = dot(pan_split[0:3].reshape(1536, 2048), inv_split[0, 3])
+        rest = dot(pan_split[0:3, 0:256, :].reshape(768, 2048), inv_split[1, 3])
+        for g in range(3):
+            finish(g, 3, *join(both[g * 512:(g + 1) * 512], rest[g * 256:(g + 1) * 256]))
 
     def loop(begin, end, body):
         def step(i, _):
@@ -313,29 +327,45 @@
                 columns = slice(j * TILE, (j + 1) * TILE)
                 pan[ri, rows, columns] = value[:, columns] * mask[g // 2][j]
     pl.semaphore_wait(barrier, len(greeted))
-    direct(0)
-    direct(1)
+    direct_inv(0)
+    send_pan(0)
+    send_pan(1)
+    direct_inv(1)
+    direct_inv(2)
+    direct_inv(3)
     own_inv.wait()
     for part in range(PARTS):
         split_inv(part, y)
         split_left(part, l, pan)
     pass_on(0)
-    direct(2)
+    inv_on(0)
+    send_pan(2)
     pass_on(1)
+    inv_on(1)
     pass_same(0)
-    direct(3)
+    send_pan(3)
+    marks = [len(waits)]
     pass_on(2)
+    inv_on(2)
     pass_same(1)
     near(0)
     far(0)
+    inv_on(3)
+    inv_done(0)
     corner(0)
+    marks.append(len(waits))
     pass_on(3)
     pass_same(2)
     near(1)
     far(1)
+    inv_done(1)
     corner(1)
+    flush(marks[0])
     near(2)
     far(2)
+    inv_done(2)
+    marks.append(len(waits) - marks[0])
+    pass_same(3)
     corner(2)
 
     rows_first = pl.ds(pl.multiple_of(p * 48, 16), 48)
@@ -347,40 +377,44 @@
     def last_of(p_):
         return pl.ds(pl.multiple_of(192 + p_ * 16, 16), 16)
 
-    for p_ in poles:
-        send(real_part.at[:, first_of(p_), 0:384], early.at[p], early_recv.at[p], at(p_, h, c, y, l))
-    pass_same(3)
-    near(3)
-    there, missing = [wrap(h - 1 + l), wrap(h + l)], [wrap(h + 1 + l), wrap(h + 2 + l)]
-    loop(0, 3, lambda i: begin_block(i, 3, i, there))
-    loop(0, 3, lambda i: begin_block(3 + i, i, 3, [wrap(y - 1), y, wrap(y + 1)]))
-    early_sum[...] = real_part[:, rows_first, 0:384]
-    for p_ in poles:
-        arrived(early.at[p_], early_recv.at[p_])
-        early_sum[...] += early[p_]
-    send(early_sum.at[1 - l], early_other, other_recv, partner)
-    far(3)
-    loop(0, 3, lambda i: end_block(i, 3, i, missing))
-    loop(0, 3, lambda i: end_block(3 + i, i, 3, [wrap(y + 2)]))
-    multiply(3, 3)
+    def send_early(k):
+        columns = (slice(0, 384), slice(384, 512))[k]
+        for p_ in poles:
+            send(real_part.at[:, first_of(p_), columns], early.at[p, :, :, columns], early_recv.at[p, k],
+                 at(p_, h, c, y, l))
 
     here = ((7 - row) // 7).astype(F32)
-    for o in (0, 1):
-        k = l if o == 0 else 1 - l
-        both = dot(left_split[k], right_split[k, 0])
-        both = both[0:256] + both[256:512] + dot(left_split[k, 0:256, :], right_split[k, 1])
-        for half in (0, 1):
-            inner = slice(half * TILE, (half + 1) * TILE)
-            tile = both[inner, inner]
+
+    def couple(half):
+        rows = slice(half * TILE, (half + 1) * TILE)
+        low_rows = slice(256 + half * TILE, 256 + (half + 1) * TILE)
+        for o in (0, 1):
+            k = l if o == 0 else 1 - l
+            high = left_split[k, rows, :]
+            tile = dot(high, right_split[k, 0, rows, :]) + dot(high, right_split[k, 1, rows, :])
+            tile += dot(left_split[k, low_rows, :], right_split[k, 0, rows, :])
             if o == 0:
                 tile += here * (real_weight * diag[0, half, 0] - imag_weight * diag[0, half, 1])
             tile_part[k, half] = tile
+
+    send_early(0)
+    inv_done(3)
+    multiply_tall()
+    send_early(1)
+    couple(0)
+    near(3)
+    far(3)
+    loop(0, 2, multiply_wide)
+    couple(1)
     send(tile_part.at[:, 1 - c], tile_other, core_recv, sibling)
+    early_sum[...] = real_part[:, rows_first, :]
+    for p_ in poles:
+        arrived(early.at[p_, :, :, 0:384], early_recv.at[p_, 0])
+        arrived(early.at[p_, :, :, 384:512], early_recv.at[p_, 1])
+        early_sum[...] += early[p_]
+    send(early_sum.at[1 - l], early_other, other_recv, partner)
 
     me = 2 * p + l
-    for p_, l_ in reducers:
-        send(real_part.at[l_, last_of(p_), :], late_rows.at[me], rows_recv.at[me], at(p_, h, c, y, l_))
-        send(real_part.at[l_, first_of(p_), 384:512], late_cols.at[me], cols_recv.at[me], at(p_, h, c, y, l_))
 
     def piece(p_):
         return pl.ds(pl.multiple_of(p_ * 32, 32), 32)
@@ -397,32 +431,31 @@
     tile_sum[...] = tile_part[:, c] + tile_other[...]
     for p_, l_ in reducers:
         send(tile_sum.at[l_, piece(p_), :], tile_pieces.at[me], piece_recv.at[me], at(p_, h, c, y, l_))
+    for p_, l_ in reducers:
+        send(real_part.at[l_, last_of(p_), :], late_rows.at[me], rows_recv.at[me], at(p_, h, c, y, l_))
+    flush(marks[2])
     arrived(early_other, other_recv)
 
-    def masked(total, begin, columns):
+    def masked(total, begin):
         upper = begin // TILE
-        for j in columns:
-            wide = slice((j - columns[0]) * TILE, (j - columns[0] + 1) * TILE)
+        for j in range(4):
+            columns = slice(j * TILE, (j + 1) * TILE)
             factor = jnp.where(upper == 0, mask[0][j], mask[1][j])
-            dens[pl.ds(pl.multiple_of(begin, 16), 16), j * TILE:(j + 1) * TILE] = -factor * total[:, wide]
+            dens[pl.ds(pl.multiple_of(begin, 16), 16), columns] = -factor * total[:, columns]
 
     for s in range(3):
         inner = slice(s * 16, (s + 1) * 16)
-        masked(early_sum[l, inner, :] + early_other[inner, :], p * 48 + s * 16, (0, 1, 2))
+        masked(early_sum[l, inner, :] + early_other[inner, :], p * 48 + s * 16)
     for p_ in poles:
-        send(dens.at[rows_first, 0:384], dens.at[rows_first, 0:384], out_recv.at[p, 0], at(p_, h, c, y, l))
+        send(dens.at[rows_first, :], dens.at[rows_first, :], out_recv.at[p, 0], at(p_, h, c, y, l))
 
     tile_rows[h] = collect(tile_sum[l, piece(p), :], tile_pieces, piece_recv)
     for h_ in heights:
         send(tile_rows.at[h], tile_rows.at[h], part_recv.at[h], at(p, h_, c, y, l))
-    masked(collect(real_part[l, rows_last, :], late_rows, rows_recv), 192 + p * 16, (0, 1, 2, 3))
+    masked(collect(real_part[l, rows_last, :], late_rows, rows_recv), 192 + p * 16)
     for p_ in poles:
         send(dens.at[rows_last, :], dens.at[rows_last, :], out_recv.at[p, 1], at(p_, h, c, y, l))
-    total = collect(real_part[l, rows_first, 384:512], late_cols, cols_recv)
-    for s in range(3):
-        masked(total[s * 16:(s + 1) * 16], p * 48 + s * 16, (3,))
-    for p_ in poles:
-        send(dens.at[rows_first, 384:512], dens.at[rows_first, 384:512], out_recv.at[p, 2], at(p_, h, c, y, l))
+    flush(len(waits) - 26)
     for h_ in heights:
         arrived(tile_rows.at[h_], part_recv.at[h_])
 
@@ -434,19 +467,13 @@
     for p_, c_ in copies:
         send(mine, mine, recv, at(p_, h, c_, y, l))
     for p_ in poles:
-        for k, target in enumerate((
-            dens.at[first_of(p_), 0:384], dens.at[last_of(p_), :], dens.at[first_of(p_), 384:512],
-        )):
-            arrived(target, out_recv.at[p_, k])
+        arrived(dens.at[first_of(p_), :], out_recv.at[p_, 0])
+        arrived(dens.at[last_of(p_), :], out_recv.at[p_, 1])
     for p_, c_ in copies:
         arrived(*tile_of(p_, c_))
     assert slots[0] <= SENDS
 
-    for flag, finish in waits:
-        if flag is None:
-            finish()
-        else:
-            pl.when(flag)(finish)
+    flush(len(waits))
 
 
 def shards(root_inverse, panel, diag_inverse, pole_weight, block_node, pattern):
@@ -467,24 +494,22 @@
             pltpu.VMEM((9, 2, 256, 512), F32),
             pltpu.VMEM((2, 4, 256, 2048), half),
             pltpu.VMEM((4, 512, 2048), half),
-            pltpu.VMEM((6, 2, TILE, 256), F32),
             pltpu.VMEM((2, 256, 512), F32),
             pltpu.VMEM((2, 512, 1024), half),
             pltpu.VMEM((2, 2, 256, 1024), half),
             pltpu.VMEM((2, 2, TILE, TILE), F32),
-            pltpu.VMEM((4, 2, 48, 384), F32),
-            pltpu.VMEM((2, 48, 384), F32),
-            pltpu.VMEM((48, 384), F32),
+            pltpu.VMEM((4, 2, 48, 512), F32),
+            pltpu.VMEM((2, 48, 512), F32),
+            pltpu.VMEM((48, 512), F32),
             pltpu.VMEM((8, 16, 512), F32),
-            pltpu.VMEM((8, 48, TILE), F32),
             pltpu.VMEM((2, TILE, TILE), F32),
             pltpu.VMEM((2, TILE, TILE), F32),
             pltpu.VMEM((8, 32, TILE), F32),
             pltpu.VMEM((4, 32, TILE), F32),
             dma((SENDS,)),
             dma((4, 2, PARTS)), dma((9, 2, PARTS)),
-            dma((4,)), dma, dma((8,)), dma((8,)), dma, dma((8,)),
-            dma((4,)), dma((4, 3)), dma((8,)), dma((2,)),
+            dma((4, 2)), dma, dma((8,)), dma, dma((8,)),
+            dma((4,)), dma((4, 2)), dma((8,)), dma((2,)),
         ],
         compiler_params=pltpu.CompilerParams(
             collective_id=0, has_side_effects=True, vmem_limit_bytes=VMEM_LIMIT

time: 133 us -> 124 us (0.932)
  Pallas kernels: 128 us -> 120 us
    pallas_call x1, Pallas kernels: 128 us -> 120 us  [shards(): pl.pallas_call(kernel, out_shape=(jax.ShapeDtypeStruct((256, 512), F32),...]
where the time goes in v4:
time: 124 us
  Pallas kernels  120 us (97%)
  local copies, waits for them, and re-layouts  3.44 us (3%)
    pallas_call x1, Pallas kernels, shards(): pl.pallas_call(kernel, out_shape=(jax.ShapeDtypeStruct((256, 512), F32),...  120 us
    unnamed x2, local copies, waits for them, and re-layouts  3.44 us

profile of v4, /device:TPU:1, one launch (start us, length us, event | category | flops | bytes accessed | tf_op | source)
XLA Modules:
  0.0 123.6 jit_solution(11950907898540137003)
XLA Ops:
  0.6 119.5 %shard_map.77 = (f32[256,512]{1,0:T(8,128)}, f32[256,128]{1,0:T(8,128)}) custom-call(f32[1,2,512,512]{3,2,1,0:T(8,128)} %inv.1, f32[1,256,2,512]{3,2,1,0:T(2,128)} %panel.1, f32[1,2,2,128,128]{4,3,2,1,0:T(8,128)} %diag.1, f32[1,2]{1,0:T(1,128)} %weight.1, s32[2]{0:T(128)} %node.1, s32[4,4]{1,0:T(4,128)} %pattern.1), custom_call_target="tpu_custom_call" | custom-call | flops 25999998976 | bytes 6000000 | tf_op jit(solution)/shard_map/pallas_call | solution.py:485
  120.1 1.9 %copy.10 = f32[256,512]{1,0:T(8,128)} copy(f32[256,512]{1,0:T(8,128)} %get-tuple-element.8) | data formatting | bytes 1048576
  122.0 1.6 %copy.11 = f32[2,128,128]{2,1,0:T(8,128)} copy(f32[2,128,128]{2,1,0:T(8,128)} %bitcast.1) | data formatting | bytes 262144

commit v5 on v4

--- a/solution.py
+++ b/solution.py
@@ -198,11 +198,15 @@
         pass_inv(part, wrap(y + 1), 1, down)
 
     def pass_same(part):
-        arrived_pan(part, same_left, c)
-        arrived_pan(part, same_right, c)
-        pass_pan(part, (1 - c) * same_left + c * same_right, at(p, wrap(h + 1 - 2 * c), c, y, l))
-        pass_pan(part, same_left, sibling)
-        pass_pan(part, same_right, sibling)
+        slot = (1 - l) * same_right + l * same_left
+        arrived_pan(part, slot, c)
+        pass_pan(part, slot, at(p, wrap(h + behind), c, y, l))
+        pass_pan(part, slot, sibling)
+
+    def take_same(part):
+        slot = l * same_right + (1 - l) * same_left
+        arrived_pan(part, slot, c)
+        pass_pan(part, slot, sibling)
 
     def direct_inv(part):
         send_inv(part, 0, up)
@@ -338,16 +342,19 @@
         split_inv(part, y)
         split_left(part, l, pan)
     pass_on(0)
+    pass_same(0)
     inv_on(0)
     send_pan(2)
     pass_on(1)
+    pass_same(1)
     inv_on(1)
-    pass_same(0)
+    take_same(0)
     send_pan(3)
     marks = [len(waits)]
     pass_on(2)
+    pass_same(2)
     inv_on(2)
-    pass_same(1)
+    take_same(1)
     near(0)
     far(0)
     inv_on(3)
@@ -355,7 +362,8 @@
     corner(0)
     marks.append(len(waits))
     pass_on(3)
-    pass_same(2)
+    pass_same(3)
+    take_same(2)
     near(1)
     far(1)
     inv_done(1)
@@ -365,8 +373,8 @@
     far(2)
     inv_done(2)
     marks.append(len(waits) - marks[0])
-    pass_same(3)
     corner(2)
+    take_same(3)
 
     rows_first = pl.ds(pl.multiple_of(p * 48, 16), 48)
     rows_last = pl.ds(pl.multiple_of(192 + p * 16, 16), 16)

time: 124 us -> 119 us (0.960)
  Pallas kernels: 120 us -> 114 us
    pallas_call x1, Pallas kernels: 120 us -> 114 us  [shards(): pl.pallas_call(kernel, out_shape=(jax.ShapeDtypeStruct((256, 512), F32),...]
where the time goes in v5:
time: 119 us; the launch traced here: 118 us
  Pallas kernels  114 us (96%)
  local copies, waits for them, and re-layouts  3.44 us (3%)
    pallas_call x1, Pallas kernels, shards(): pl.pallas_call(kernel, out_shape=(jax.ShapeDtypeStruct((256, 512), F32),...  114 us
    unnamed x2, local copies, waits for them, and re-layouts  3.44 us

profile of v5, /device:TPU:1, one launch (start us, length us, event | category | flops | bytes accessed | tf_op | source)
XLA Modules:
  0.0 118.4 jit_solution(11569722751303367120)
XLA Ops:
  0.6 114.3 %shard_map.77 = (f32[256,512]{1,0:T(8,128)}, f32[256,128]{1,0:T(8,128)}) custom-call(f32[1,2,512,512]{3,2,1,0:T(8,128)} %inv.1, f32[1,256,2,512]{3,2,1,0:T(2,128)} %panel.1, f32[1,2,2,128,128]{4,3,2,1,0:T(8,128)} %diag.1, f32[1,2]{1,0:T(1,128)} %weight.1, s32[2]{0:T(128)} %node.1, s32[4,4]{1,0:T(4,128)} %pattern.1), custom_call_target="tpu_custom_call" | custom-call | flops 25999998976 | bytes 6000000 | tf_op jit(solution)/shard_map/pallas_call | solution.py:493
  115.0 1.9 %copy.10 = f32[256,512]{1,0:T(8,128)} copy(f32[256,512]{1,0:T(8,128)} %get-tuple-element.8) | data formatting | bytes 1048576
  116.8 1.6 %copy.11 = f32[2,128,128]{2,1,0:T(8,128)} copy(f32[2,128,128]{2,1,0:T(8,128)} %bitcast.1) | data formatting | bytes 262144

commit v6 on v5

--- a/solution.py
+++ b/solution.py
@@ -322,18 +322,23 @@
         if part:
             loop(0, part, lambda i: multiply(i, part))
 
-    raw_copy.wait()
-    for g in range(PARTS):
+    def lay_out(g):
         rows = slice(g * 64, (g + 1) * 64)
         for ri in (0, 1):
             value = raw[rows, ri, :]
             for j in range(4):
                 columns = slice(j * TILE, (j + 1) * TILE)
                 pan[ri, rows, columns] = value[:, columns] * mask[g // 2][j]
+
+    raw_copy.wait()
+    lay_out(0)
     pl.semaphore_wait(barrier, len(greeted))
+    send_pan(0)
     direct_inv(0)
-    send_pan(0)
-    send_pan(1)
+    for part in range(1, PARTS):
+        lay_out(part)
+        if part < 3:
+            send_pan(part)
     direct_inv(1)
     direct_inv(2)
     direct_inv(3)
@@ -344,12 +349,11 @@
     pass_on(0)
     pass_same(0)
     inv_on(0)
-    send_pan(2)
+    send_pan(3)
     pass_on(1)
     pass_same(1)
     inv_on(1)
     take_same(0)
-    send_pan(3)
     marks = [len(waits)]
     pass_on(2)
     pass_same(2)
@@ -482,6 +486,11 @@
     assert slots[0] <= SENDS
 
     flush(len(waits))
+
+
+def hand_over(dens_in, tiles_in, dens, tiles):
+    dens[...] = dens_in[...]
+    tiles[...] = tiles_in[...]
 
 
 def shards(root_inverse, panel, diag_inverse, pole_weight, block_node, pattern):
@@ -524,7 +533,12 @@
         ),
         cost_estimate=pl.CostEstimate(flops=26_000_000_000, bytes_accessed=6_000_000, transcendentals=0),
     )(root_inverse, panel, diag_inverse, pole_weight, block_node, pattern)
-    return dens, tiles.reshape(2, TILE, TILE)
+    return pl.pallas_call(
+        hand_over,
+        out_shape=(jax.ShapeDtypeStruct((256, 512), F32), jax.ShapeDtypeStruct((2, TILE, TILE), F32)),
+        in_specs=[vmem, vmem],
+        out_specs=(vmem, vmem),
+    )(dens, tiles.reshape(2, TILE, TILE))
 
 
 def solution(mesh):

time: 119 us -> 116 us (0.975)
  local copies, waits for them, and re-layouts: 3.44 us -> 0 us
    unnamed x2 -> x0, local copies, waits for them, and re-layouts: 3.44 us -> none
    pallas_call x0 -> x1, Pallas kernels: none -> 1.93 us  [shards(): pl.pallas_call(hand_over, out_shape=(jax.ShapeDtypeStruct((256, 512), F32...]
where the time goes in v6:
time: 116 us
  Pallas kernels  115 us (99%)
    pallas_call x1, Pallas kernels, shards(): pl.pallas_call(kernel, out_shape=(jax.ShapeDtypeStruct((256, 512), F32),...  113 us

profile of v6, /device:TPU:1, one launch (start us, length us, event | category | flops | bytes accessed | tf_op | source)
XLA Modules:
  0.0 115.8 jit_solution(9884027087919778668)
XLA Ops:
  0.6 113.3 %shard_map.77 = (f32[256,512]{1,0:T(8,128)}, f32[256,128]{1,0:T(8,128)}) custom-call(f32[1,2,512,512]{3,2,1,0:T(8,128)} %inv.1, f32[1,256,2,512]{3,2,1,0:T(2,128)} %panel.1, f32[1,2,2,128,128]{4,3,2,1,0:T(8,128)} %diag.1, f32[1,2]{1,0:T(1,128)} %weight.1, s32[2]{0:T(128)} %node.1, s32[4,4]{1,0:T(4,128)} %pattern.1), custom_call_target="tpu_custom_call" | custom-call | flops 25999998976 | bytes 6000000 | tf_op jit(solution)/shard_map/pallas_call | solution.py:502
  113.9 1.9 %shard_map.78 = (f32[256,512]{1,0:T(8,128)}, f32[2,128,128]{2,1,0:T(8,128)}) custom-call(f32[256,512]{1,0:T(8,128)} %get-tuple-element.4.dens_in, f32[2,128,128]{2,1,0:T(8,128)} %bitcast.1), custom_call_target="tpu_custom_call" | custom-call | tf_op jit(solution)/shard_map/pallas_call | solution.py:536

commit v7 on v6

--- a/solution.py
+++ b/solution.py
@@ -445,7 +445,6 @@
         send(tile_sum.at[l_, piece(p_), :], tile_pieces.at[me], piece_recv.at[me], at(p_, h, c, y, l_))
     for p_, l_ in reducers:
         send(real_part.at[l_, last_of(p_), :], late_rows.at[me], rows_recv.at[me], at(p_, h, c, y, l_))
-    flush(marks[2])
     arrived(early_other, other_recv)
 
     def masked(total, begin):
@@ -464,6 +463,7 @@
     tile_rows[h] = collect(tile_sum[l, piece(p), :], tile_pieces, piece_recv)
     for h_ in heights:
         send(tile_rows.at[h], tile_rows.at[h], part_recv.at[h], at(p, h_, c, y, l))
+    flush(marks[2])
     masked(collect(real_part[l, rows_last, :], late_rows, rows_recv), 192 + p * 16)
     for p_ in poles:
         send(dens.at[rows_last, :], dens.at[rows_last, :], out_recv.at[p, 1], at(p_, h, c, y, l))
@@ -488,9 +488,15 @@
     flush(len(waits))
 
 
-def hand_over(dens_in, tiles_in, dens, tiles):
-    dens[...] = dens_in[...]
-    tiles[...] = tiles_in[...]
+def hand_over(dens_in, tiles_in, dens, tiles, sems):
+    copies = [
+        pltpu.make_async_copy(dens_in, dens, sems.at[0]),
+        pltpu.make_async_copy(tiles_in, tiles, sems.at[1]),
+    ]
+    for copy in copies:
+        copy.start()
+    for copy in copies:
+        copy.wait()
 
 
 def shards(root_inverse, panel, diag_inverse, pole_weight, block_node, pattern):
@@ -537,7 +543,8 @@
         hand_over,
         out_shape=(jax.ShapeDtypeStruct((256, 512), F32), jax.ShapeDtypeStruct((2, TILE, TILE), F32)),
         in_specs=[vmem, vmem],
-        out_specs=(vmem, vmem),
+        out_specs=(hbm, hbm),
+        scratch_shapes=[dma((2,))],
     )(dens, tiles.reshape(2, TILE, TILE))
 
 

time: 116 us -> 116 us (level)
  no operation moved by 1% of the time
where the time goes in v7:
time: 116 us
  Pallas kernels  115 us (99%)
    pallas_call x1, Pallas kernels, shards(): pl.pallas_call(kernel, out_shape=(jax.ShapeDtypeStruct((256, 512), F32),...  113 us

profile of v7, /device:TPU:1, one launch (start us, length us, event | category | flops | bytes accessed | tf_op | source)
XLA Modules:
  0.0 116.0 jit_solution(4209821241989107613)
XLA Ops:
  0.6 113.3 %shard_map.77 = (f32[256,512]{1,0:T(8,128)}, f32[256,128]{1,0:T(8,128)}) custom-call(f32[1,2,512,512]{3,2,1,0:T(8,128)} %inv.1, f32[1,256,2,512]{3,2,1,0:T(2,128)} %panel.1, f32[1,2,2,128,128]{4,3,2,1,0:T(8,128)} %diag.1, f32[1,2]{1,0:T(1,128)} %weight.1, s32[2]{0:T(128)} %node.1, s32[4,4]{1,0:T(4,128)} %pattern.1), custom_call_target="tpu_custom_call" | custom-call | flops 25999998976 | bytes 6000000 | tf_op jit(solution)/shard_map/pallas_call | solution.py:508
  113.9 1.9 %shard_map.78 = (f32[256,512]{1,0:T(8,128)}, f32[2,128,128]{2,1,0:T(8,128)}) custom-call(f32[256,512]{1,0:T(8,128)} %get-tuple-element.4.dens_in, f32[2,128,128]{2,1,0:T(8,128)} %bitcast.1), custom_call_target="tpu_custom_call" | custom-call | tf_op jit(solution)/shard_map/pallas_call | solution.py:542
